TPU v7x, 128 devices: a whole 4x4x4 slice. The times are simulated.
128 devices in a mesh: band: 32 (over z, x, core), sub: 4 (over y).
Axes of the slice: x: 4, y: 4, z: 4, core: 2. Of those that a mesh axis runs over, the one named last changes fastest.
Arguments:
- level_set: float32 [8, 8, 8, 65536], P(None, None, None, ('band', 'sub')), may hold values from -6 to 6
- velocity: float32 [3, 8, 8, 8, 65536], P(None, None, None, None, ('band', 'sub')), may hold values from -3 to 3
- neighbours: int32 [6, 65536], P(None, ('band', 'sub')), may hold values from -1 to 65535, as said below
Outputs:
- advected: float32 [8, 8, 8, 65536], P(None, None, None, ('band', 'sub'))
- reinitialized: float32 [8, 8, 8, 65536], P(None, None, None, ('band', 'sub'))
Inputs may be any that keep to these rules, and one draw needn't show every extreme that they name: `neighbours`: links are symmetric (if tile a is the +x neighbour of b then b is the -x neighbour of a, likewise for y and z). Tile t lives on device t // 512 of the flattened band+sub order. An x neighbour is on the same device or on the device whose band index is one less (for -x) or one more (for +x) with the same sub index; a y neighbour likewise on sub index one less or one more with the same band index; a z neighbour always on the same device. Between two devices adjacent along band there are exactly 16 * 16 x links, along sub exactly 2 * 16 y links.
All inputs are finite; a program needn't handle non-finite values. Where the computation divides by a largest or mean magnitude, that divisor is 1e-20 or more.
Results may differ from a plain program's by a relative error of at most 0.0003.
Values sent between devices are 32-bit elements; how exact they have to be, the bound alone decides.
A program may use at most 64 MiB of HBM per device.

v0:
```python
import functools

import jax
import jax.numpy as jnp
from jax import lax
from jax.experimental import pallas as pl
from jax.experimental.pallas import tpu as pltpu
from jax.sharding import PartitionSpec as P

TILES_DEV = 512
SLOTS_X = 256
SLOTS_Y = 128
FACE = 192
STAGES = 3
REINIT = 2
STEPS = STAGES + REINIT
EPS = 1e-06
CFL = 0.5
DTAU = 0.3
ROOT_EPS = 1e-06
LANES = 128
GROUPS = TILES_DEV // LANES

F32 = jnp.float32
BF16 = jnp.bfloat16
MESH = pl.DeviceIdType.MESH


def differences(p):
    first = [p[k + 1] - p[k] for k in range(13)]
    second = [first[k + 1] - first[k] for k in range(12)]
    third = [second[k + 1] - second[k] for k in range(11)]
    fourth = [None] + [third[k] - third[k - 1] for k in range(1, 11)]
    square = [e * e for e in second]
    ind_a, ind_b, ind_c = {}, {}, {}
    for k in range(11):
        half = (0.5 * second[k]) * second[k + 1]
        base = third[k] * third[k] * (2.0 / 3.0) + 0.5 * EPS
        low = base - half
        if k <= 8:
            ind_a[k] = low + square[k + 1]
        if 1 <= k <= 9:
            ind_b[k] = base + half
        if k >= 2:
            ind_c[k] = low + square[k]
    return third, fourth, ind_a, ind_b, ind_c


def recip(x):
    return pl.reciprocal(x, approx=True)


def advect_line(p, flow):
    third, fourth, ind_a, ind_b, ind_c = differences(p)
    out = []
    for c in range(8):
        up = flow[c] > 0
        ra = recip(jnp.where(up, ind_a[c], ind_c[c + 3]))
        rb = recip(jnp.where(up, ind_b[c + 1], ind_b[c + 2]))
        rc = recip(jnp.where(up, ind_c[c + 2], ind_a[c + 1]))
        wa = ra * ra
        wb = rb * rb * 6.0
        wc = rc * rc * 3.0
        far = jnp.where(up, fourth[c + 1], fourth[c + 3])
        num = wa * (far + far) + wc * fourth[c + 2]
        corr = num * recip(wa + wb + wc)
        linear = 3.0 * (p[c + 4] - p[c + 2]) - jnp.where(up, third[c + 1], third[c + 2])
        out.append(flow[c] * linear - jnp.abs(flow[c]) * corr)
    return out


def reinit_line(p, sign):
    third, fourth, ind_a, ind_b, ind_c = differences(p)
    wa, wa3, wb, wc, wc3 = {}, {}, {}, {}, {}
    for k, v in ind_a.items():
        r = recip(v)
        wa[k] = r * r
        wa3[k] = wa[k] * 3.0
    for k, v in ind_b.items():
        r = recip(v)
        wb[k] = r * r * 6.0
    for k, v in ind_c.items():
        r = recip(v)
        wc[k] = r * r
        wc3[k] = wc[k] * 3.0
    twice = [None] + [f + f for f in fourth[1:]]
    out = []
    for c in range(8):
        linear = 3.0 * (p[c + 4] - p[c + 2])
        corr_b = (wa[c] * twice[c + 1] + wc3[c + 2] * fourth[c + 2]) * recip(wa[c] + wb[c + 1] + wc3[c + 2])
        corr_f = (wc[c + 3] * twice[c + 3] + wa3[c + 1] * fourth[c + 2]) * recip(wc[c + 3] + wb[c + 2] + wa3[c + 1])
        back = linear - third[c + 1] - corr_b
        fore = third[c + 2] - linear - corr_f
        m = jnp.maximum(jnp.maximum(sign[c] * back, sign[c] * fore), 0.0)
        out.append(m * m)
    return out


def split_rows(value):
    hi = value.astype(BF16)
    lo = (value - hi.astype(F32)).astype(BF16)
    return hi, lo


def kernel(
    n_band, n_sub, group,
    ls_ref, vel_ref, nb_ref, adv_out, out_ref,
    p0, pc, adv, sgn, vel, az, ay, halo, faces, local_m, pack_x, pack_y, unpack_x, unpack_y, tri, pres,
    nb_s, ids_s, krow, kcol, send_x, send_y, recv_x, recv_y, ar_send, ar_sub, ar_grp, ar_z, step_s,
    in_sem, out_sem, tx_sem, rx_sem, ar_tx, ar_rx,
):
    band = lax.axis_index("band")
    sub = lax.axis_index("sub")
    n_z = n_band // group
    band_up, band_dn = lax.rem(band + 1, n_band), lax.rem(band + n_band - 1, n_band)
    sub_up, sub_dn = lax.rem(sub + 1, n_sub), lax.rem(sub + n_sub - 1, n_sub)
    first_of_group = band - lax.rem(band, group)

    def sub_peer(d):
        return (band, lax.rem(sub + d, n_sub))

    def group_peer(d):
        return (first_of_group + lax.rem(lax.rem(band, group) + d, group), sub)

    def z_peer(d):
        return (lax.rem(band + d * group, n_band), sub)

    def lanes(g):
        return pl.ds(g * LANES, LANES)

    in_copies = []
    for g in range(GROUPS):
        in_copies.append(pltpu.make_async_copy(ls_ref.at[:, :, lanes(g)], p0.at[g], in_sem.at[g]))
    for k in range(3):
        for g in range(GROUPS):
            in_copies.append(
                pltpu.make_async_copy(vel_ref.at[k, :, :, lanes(g)], vel.at[k, g], in_sem.at[4 + 4 * k + g])
            )
    for copy in in_copies:
        copy.start()

    peers = [(band_up, sub), (band_dn, sub)]
    peers += [sub_peer(d) for d in range(1, n_sub)]
    peers += [group_peer(d) for d in range(1, group)]
    peers += [z_peer(d) for d in range(1, n_z)]
    barrier = pltpu.get_barrier_semaphore()
    for peer in peers:
        pl.semaphore_signal(barrier, inc=1, device_id=peer, device_id_type=MESH)

    nb_s[...] = jnp.full((8, TILES_DEV), -1, jnp.int32)
    nb_s[0:6, :] = nb_ref[...]
    nb = nb_s[...]
    base = (band * n_sub + sub) * TILES_DEV
    present = nb >= 0
    is_local = (nb >= base) & (nb < base + TILES_DEV)
    remote = present & jnp.logical_not(is_local)
    ids_s[0] = jnp.where(is_local, nb - base, -1)
    presf = jnp.where(present, 1.0, 0.0)
    for d in range(6):
        for g in range(GROUPS):
            pres[d, g] = jnp.broadcast_to(presf[d : d + 1, g * LANES : (g + 1) * LANES], (16, LANES))

    def fill(k, carry):
        rows = pl.ds(pl.multiple_of(16 * k, 16), 16)
        iota = lax.broadcasted_iota(jnp.int32, (16, TILES_DEV), 0) + 16 * k
        for d in range(6):
            local_m[d, rows, :] = jnp.where(iota == ids_s[0, d : d + 1, :], 1.0, 0.0).astype(BF16)
        lane = lax.broadcasted_iota(jnp.int32, (16, TILES_DEV), 1)
        tri[rows, :] = jnp.where(iota < lane, 1.0, 0.0).astype(BF16)
        return carry

    lax.fori_loop(0, TILES_DEV // 16, fill, 0)

    flags = jnp.where(remote, 1.0, 0.0)
    flags16 = jnp.concatenate([flags, jnp.zeros_like(flags)], axis=0).astype(BF16)
    place = jnp.dot(flags16, tri[...], preferred_element_type=F32)[0:8]
    keys = jnp.where(remote, nb.astype(F32), 1e9)
    krow[...] = jnp.zeros_like(krow)
    krow[0:4, :] = keys[0:4]
    krow[4:8, :] = jnp.where(remote, place, -1.0)[0:4]
    for c in range(GROUPS):
        kcol[c * LANES : (c + 1) * LANES, :] = krow[:, c * LANES : (c + 1) * LANES].T

    def count(k, carry):
        rows = pl.ds(pl.multiple_of(8 * k, 8), 8)
        return tuple(
            total + jnp.where(kcol[rows, d : d + 1] < krow[d : d + 1, :], 1.0, 0.0) for d, total in enumerate(carry)
        )

    zero = jnp.zeros((8, TILES_DEV), F32)
    counts = lax.fori_loop(0, TILES_DEV // 8, count, (zero,) * 4)
    for d in range(4):
        rank = jnp.sum(counts[d], axis=0, keepdims=True).astype(jnp.int32)
        ids_s[1, d : d + 1, :] = jnp.where(remote[d : d + 1], rank, -1)

    def fill_pack(k, carry):
        rows = pl.ds(pl.multiple_of(16 * k, 16), 16)
        lane_x = lax.broadcasted_iota(jnp.int32, (16, SLOTS_X), 1).astype(F32)
        lane_y = lax.broadcasted_iota(jnp.int32, (16, SLOTS_Y), 1).astype(F32)
        for d in range(2):
            pack_x[d, rows, :] = jnp.where(kcol[rows, 4 + d : 5 + d] == lane_x, 1.0, 0.0).astype(BF16)
            pack_y[d, rows, :] = jnp.where(kcol[rows, 6 + d : 7 + d] == lane_y, 1.0, 0.0).astype(BF16)
        return carry

    lax.fori_loop(0, TILES_DEV // 16, fill_pack, 0)

    def fill_unpack(d, dest):
        def body(k, carry):
            rows = pl.ds(pl.multiple_of(16 * k, 16), 16)
            iota = lax.broadcasted_iota(jnp.int32, (16, TILES_DEV), 0) + 16 * k
            dest[d % 2, rows, :] = jnp.where(iota == ids_s[1, d : d + 1, :], 1.0, 0.0).astype(BF16)
            return carry

        lax.fori_loop(0, dest.shape[1] // 16, body, 0)

    for d in range(4):
        fill_unpack(d, unpack_x if d < 2 else unpack_y)

    for copy in in_copies[:GROUPS]:
        copy.wait()

    def copy_in(x, carry):
        for g in range(GROUPS):
            pc[g, x] = p0[g, x]
        return carry

    lax.fori_loop(0, 8, copy_in, 0)
    for copy in in_copies[GROUPS:]:
        copy.wait()

    def speeds(idx, top):
        g, x = idx // 8, lax.rem(idx, 8)
        for y in range(8):
            rows = slice(8 * y, 8 * y + 8)
            total = jnp.abs(vel[0, g, x, rows, :]) + jnp.abs(vel[1, g, x, rows, :]) + jnp.abs(vel[2, g, x, rows, :])
            top = jnp.maximum(top, total)
        turned = [vel[2, g, x, pl.ds(z, 8, stride=8), :] for z in range(8)]
        for z in range(8):
            az[g, x, 8 * z : 8 * z + 8, :] = turned[z]
        return top

    top = lax.fori_loop(0, GROUPS * 8, speeds, jnp.zeros((8, LANES), F32))

    def turn_back(idx, carry):
        g, x = idx // 8, lax.rem(idx, 8)
        vel[2, g, x] = az[g, x]
        return carry

    lax.fori_loop(0, GROUPS * 8, turn_back, 0)

    pl.semaphore_wait(barrier, len(peers))

    def ar_copies(r):
        peer, slots, n = ((sub_peer, ar_sub, n_sub), (group_peer, ar_grp, group), (z_peer, ar_z, n_z))[r]
        first = (0, n_sub, n_sub + group)[r]
        return [
            pltpu.make_async_remote_copy(
                src_ref=ar_send.at[r],
                dst_ref=slots.at[d - 1],
                send_sem=ar_tx.at[first + d - 1],
                recv_sem=ar_rx.at[first + d - 1],
                device_id=peer(d),
                device_id_type=MESH,
            )
            for d in range(1, n)
        ], slots

    def ar_start(r, value):
        ar_send[r] = value
        for copy in ar_copies(r)[0]:
            copy.start()

    def ar_finish(r):
        value = ar_send[r]
        copies, slots = ar_copies(r)
        for k, copy in enumerate(copies):
            copy.wait()
            value = jnp.maximum(value, slots[k])
        return value

    ar_start(0, top)

    def exchange(t):
        targets = [(band_dn, sub), (band_up, sub), (band, sub_dn), (band, sub_up)]
        copies = []
        for d in range(4):
            src, dst = (send_x, recv_x) if d < 2 else (send_y, recv_y)
            copies.append(
                pltpu.make_async_remote_copy(
                    src_ref=src.at[d % 2],
                    dst_ref=dst.at[t, 1 - d % 2],
                    send_sem=tx_sem.at[d],
                    recv_sem=rx_sem.at[t, d],
                    device_id=targets[d],
                    device_id_type=MESH,
                )
            )
        return copies

    def put_face(d, row, g, value):
        hi, lo = split_rows(value)
        col = pl.ds(pl.multiple_of(g * LANES, LANES), LANES)
        faces[d, pl.ds(pl.multiple_of(row, 16), 16), col] = hi
        faces[d, pl.ds(pl.multiple_of(row + FACE, 16), 16), col] = lo

    def faces_x():
        def body(idx, carry):
            g, r = idx // 4, lax.rem(idx, 4)
            rows = pl.ds(pl.multiple_of(16 * r, 16), 16)
            for d, start in ((0, 5), (1, 0)):
                for l in range(3):
                    put_face(d, 64 * l + 16 * r, g, pc[g, start + l, rows, :])
            return carry

        lax.fori_loop(0, 4 * GROUPS, body, 0)

    def faces_y():
        def body(idx, carry):
            g, i = idx // 4, lax.rem(idx, 4)
            for d, start in ((2, 5), (3, 0)):
                for l in range(3):
                    y = start + l
                    value = pc[g, pl.ds(2 * i, 2), 8 * y : 8 * y + 8, :].reshape(16, LANES)
                    put_face(d, 64 * l + 16 * i, g, value)
            return carry

        lax.fori_loop(0, 4 * GROUPS, body, 0)

    def turned_pair(ref, g, i, k):
        return jnp.concatenate([ref[g, 2 * i + j, pl.ds(k, 8, stride=8), :] for j in range(2)], axis=0)

    def faces_z():
        def body(idx, carry):
            g, i = idx // 4, lax.rem(idx, 4)
            for d, start in ((4, 5), (5, 0)):
                for l in range(3):
                    put_face(d, 64 * l + 16 * i, g, turned_pair(pc, g, i, start + l))
            return carry

        lax.fori_loop(0, 4 * GROUPS, body, 0)

    def two_part_dot(lhs, rhs):
        res = jnp.dot(lhs, rhs, preferred_element_type=F32)
        return res[:FACE] + res[FACE:]

    def gather(d):
        res = two_part_dot(faces[d], local_m[d])
        for g in range(GROUPS):
            halo[d, g] = res[:, g * LANES : (g + 1) * LANES]

    def unpack(d, t):
        block = recv_x[t, d] if d < 2 else recv_y[t, d - 2]
        hi, lo = split_rows(block)
        matrix = unpack_x[d] if d < 2 else unpack_y[d - 2]
        res = two_part_dot(jnp.concatenate([hi, lo], axis=0), matrix)
        for g in range(GROUPS):
            halo[d, g] = halo[d, g] + res[:, g * LANES : (g + 1) * LANES]

    def padded(d, g, row, cells):
        rows = [pl.ds(pl.multiple_of(64 * l + row, 16), 16) for l in range(3)]
        there_lo = pres[d, g] > 0
        there_hi = pres[d + 1, g] > 0
        low = [jnp.where(there_lo, halo[d, g, rows[l], :], cells[0]) for l in range(3)]
        high = [jnp.where(there_hi, halo[d + 1, g, rows[l], :], cells[7]) for l in range(3)]
        return low + cells + high

    def pair(ref, g, i, k):
        return ref[g, pl.ds(2 * i, 2), 8 * k : 8 * k + 8, :].reshape(16, LANES)

    def z_lines(line, extra, g, i):
        cells = [turned_pair(pc, g, i, z) for z in range(8)]
        for z, value in enumerate(line(padded(4, g, 16 * i, cells), extra(g, i))):
            az[g, pl.ds(2 * i, 2), 8 * z : 8 * z + 8, :] = value.reshape(2, 8, LANES)

    def y_lines(line, extra, g, i):
        cells = [pair(pc, g, i, y) for y in range(8)]
        for y, value in enumerate(line(padded(2, g, 16 * i, cells), extra(g, i))):
            ay[g, pl.ds(2 * i, 2), 8 * y : 8 * y + 8, :] = (value + turned_pair(az, g, i, y)).reshape(2, 8, LANES)

    def x_lines(line, extra, finish, g, r):
        rows = pl.ds(pl.multiple_of(16 * r, 16), 16)
        cells = [pc[g, x, rows, :] for x in range(8)]
        for x, value in enumerate(line(padded(0, g, 16 * r, cells), extra(g, rows))):
            finish(g, x, rows, cells[x], value + ay[g, x, rows, :])

    def begin(t):
        faces_x()
        copies = exchange(t)
        send_x[0] = two_part_dot(faces[1], pack_x[0])
        copies[0].start()
        send_x[1] = two_part_dot(faces[0], pack_x[1])
        copies[1].start()
        faces_y()
        send_y[0] = two_part_dot(faces[3], pack_y[0])
        copies[2].start()
        send_y[1] = two_part_dot(faces[2], pack_y[1])
        copies[3].start()
        faces_z()
        gather(4)
        gather(5)
        return copies

    def run(t, line, extra_z, extra_y, extra_x, finish, after_z=None, after_y=None):
        copies = begin(t)

        def z_body(k, carry):
            gather(k)
            for i in range(4):
                z_lines(line, extra_z, k, i)
            return carry

        lax.fori_loop(0, 4, z_body, 0)
        if after_z is not None:
            after_z()
        copies[2].wait_recv()
        copies[3].wait_recv()
        unpack(2, t)
        unpack(3, t)

        def y_body(k, carry):
            y_lines(line, extra_y, k // 4, lax.rem(k, 4))
            return carry

        lax.fori_loop(0, 4 * GROUPS, y_body, 0)
        if after_y is not None:
            after_y()
        copies[0].wait_recv()
        copies[1].wait_recv()
        unpack(0, t)
        unpack(1, t)

        def x_body(k, carry):
            x_lines(line, extra_x, finish, k // 4, lax.rem(k, 4))
            return carry

        lax.fori_loop(0, 4 * GROUPS, x_body, 0)
        for copy in copies:
            copy.wait_send()

    def advect_step(t, carry):
        def after_z():
            @pl.when(t == 0)
            def _():
                ar_start(1, ar_finish(0))

        def after_y():
            @pl.when(t == 0)
            def _():
                ar_start(2, ar_finish(1))
                top = ar_finish(2)
                top = jnp.max(jnp.max(top, axis=1, keepdims=True), axis=0, keepdims=True)
                step_s[...] = jnp.broadcast_to((CFL / 6.0) / top, (16, LANES))

        old = jnp.where(t == 0, 0.0, jnp.where(t == 1, 0.75, 1.0 / 3.0))
        new = jnp.where(t == 0, 1.0, jnp.where(t == 1, 0.25, 2.0 / 3.0))

        def finish(g, x, rows, cell, total):
            value = old * p0[g, x, rows, :] + new * (cell - step_s[...] * total)
            pc[g, x, rows, :] = value
            adv[g, x, rows, :] = value
            sgn[g, x, rows, :] = jnp.where(value > 0, 1.0, -1.0)

        run(
            t,
            advect_line,
            lambda g, i: [pair(vel.at[2], g, i, z) for z in range(8)],
            lambda g, i: [pair(vel.at[1], g, i, y) for y in range(8)],
            lambda g, rows: [vel[0, g, x, rows, :] for x in range(8)],
            finish,
            after_z,
            after_y,
        )
        return carry

    lax.fori_loop(0, STAGES, advect_step, 0)

    adv_copies = [
        pltpu.make_async_copy(adv.at[g], adv_out.at[:, :, lanes(g)], out_sem.at[g]) for g in range(GROUPS)
    ]
    for copy in adv_copies:
        copy.start()

    def reinit_step(k, carry):
        def finish(g, x, rows, cell, total):
            v = adv[g, x, rows, :]
            sign = v * lax.rsqrt(v * v + 1.0)
            root = total * (1.0 / 36.0) + ROOT_EPS
            pc[g, x, rows, :] = cell + (DTAU * sign) * (1.0 - root * lax.rsqrt(root))

        run(
            STAGES + k,
            reinit_line,
            lambda g, i: [turned_pair(sgn, g, i, z) for z in range(8)],
            lambda g, i: [pair(sgn, g, i, y) for y in range(8)],
            lambda g, rows: [sgn[g, x, rows, :] for x in range(8)],
            finish,
        )
        return carry

    lax.fori_loop(0, REINIT, reinit_step, 0)

    out_copies = [
        pltpu.make_async_copy(pc.at[g], out_ref.at[:, :, lanes(g)], out_sem.at[GROUPS + g]) for g in range(GROUPS)
    ]
    for copy in out_copies:
        copy.start()
    for copy in adv_copies + out_copies:
        copy.wait()


def solution(mesh):
    n_band, n_sub = mesh.shape["band"], mesh.shape["sub"]
    group = min(8, n_band)
    n_z = n_band // group
    cells = (GROUPS, 8, 64, LANES)

    def local(level_set, velocity, neighbours):
        whole = jax.ShapeDtypeStruct((8, 64, TILES_DEV), F32)
        anywhere = pl.BlockSpec(memory_space=pl.ANY)
        advected, reinitialized = pl.pallas_call(
            functools.partial(kernel, n_band, n_sub, group),
            out_shape=(whole, whole),
            in_specs=[anywhere, anywhere, pl.BlockSpec(memory_space=pltpu.VMEM)],
            out_specs=(anywhere, anywhere),
            scratch_shapes=[
                pltpu.VMEM(cells, F32),
                pltpu.VMEM(cells, F32),
                pltpu.VMEM(cells, F32),
                pltpu.VMEM(cells, F32),
                pltpu.VMEM((3,) + cells, F32),
                pltpu.VMEM(cells, F32),
                pltpu.VMEM(cells, F32),
                pltpu.VMEM((6, GROUPS, FACE, LANES), F32),
                pltpu.VMEM((6, 2 * FACE, TILES_DEV), BF16),
                pltpu.VMEM((6, TILES_DEV, TILES_DEV), BF16),
                pltpu.VMEM((2, TILES_DEV, SLOTS_X), BF16),
                pltpu.VMEM((2, TILES_DEV, SLOTS_Y), BF16),
                pltpu.VMEM((2, SLOTS_X, TILES_DEV), BF16),
                pltpu.VMEM((2, SLOTS_Y, TILES_DEV), BF16),
                pltpu.VMEM((TILES_DEV, TILES_DEV), BF16),
                pltpu.VMEM((6, GROUPS, 16, LANES), F32),
                pltpu.VMEM((8, TILES_DEV), jnp.int32),
                pltpu.VMEM((2, 8, TILES_DEV), jnp.int32),
                pltpu.VMEM((LANES, TILES_DEV), F32),
                pltpu.VMEM((TILES_DEV, LANES), F32),
                pltpu.VMEM((2, FACE, SLOTS_X), F32),
                pltpu.VMEM((2, FACE, SLOTS_Y), F32),
                pltpu.VMEM((STEPS, 2, FACE, SLOTS_X), F32),
                pltpu.VMEM((STEPS, 2, FACE, SLOTS_Y), F32),
                pltpu.VMEM((3, 8, LANES), F32),
                pltpu.VMEM((max(1, n_sub - 1), 8, LANES), F32),
                pltpu.VMEM((max(1, group - 1), 8, LANES), F32),
                pltpu.VMEM((max(1, n_z - 1), 8, LANES), F32),
                pltpu.VMEM((16, LANES), F32),
                pltpu.SemaphoreType.DMA((16,)),
                pltpu.SemaphoreType.DMA((2 * GROUPS,)),
                pltpu.SemaphoreType.DMA((4,)),
                pltpu.SemaphoreType.DMA((STEPS, 4)),
                pltpu.SemaphoreType.DMA((n_sub + group + n_z,)),
                pltpu.SemaphoreType.DMA((n_sub + group + n_z,)),
            ],
            compiler_params=pltpu.CompilerParams(
                collective_id=0, has_side_effects=True, vmem_limit_bytes=56 * 2**20
            ),
        )(level_set.reshape(8, 64, TILES_DEV), velocity.reshape(3, 8, 64, TILES_DEV), neighbours)
        return advected.reshape(8, 8, 8, TILES_DEV), reinitialized.reshape(8, 8, 8, TILES_DEV)

    return jax.shard_map(
        local,
        mesh=mesh,
        in_specs=(
            P(None, None, None, ("band", "sub")),
            P(None, None, None, None, ("band", "sub")),
            P(None, ("band", "sub")),
        ),
        out_specs=(P(None, None, None, ("band", "sub")), P(None, None, None, ("band", "sub"))),
        check_vma=False,
    )
```

profile of v0, /device:TPU:0, one launch (start us, length us, event | category | flops | bytes accessed | tf_op | source)
XLA Modules:
  0.0 86.0 jit_solution(8792529352443972338)
XLA Ops:
  0.6 80.9 %shard_map.50 = (f32[8,64,512]{2,1,0:T(8,128)}, f32[8,64,512]{2,1,0:T(8,128)}) custom-call(f32[8,64,512]{2,1,0:T(8,128)} %bitcast.7, f32[3,8,64,512]{3,2,1,0:T(8,128)} %bitcast.4, s32[6,512]{1,0:T(8,128)} %nb_ref.1), custom_call_target="tpu_custom_call" | custom-call | tf_op jit(solution)/shard_map/pallas_call | solution.py:520
  81.5 2.3 %copy.7 = f32[8,8,8,512]{3,2,1,0:T(8,128)} copy(f32[8,8,8,512]{3,2,1,0:T(8,128)} %bitcast.6) | data formatting | bytes 2097152
  83.8 2.3 %copy.8 = f32[8,8,8,512]{3,2,1,0:T(8,128)} copy(f32[8,8,8,512]{3,2,1,0:T(8,128)} %bitcast.5) | data formatting | bytes 2097152
where the time goes:
time: 86.3 us; the launch traced here: 86 us
  Pallas kernels  80.9 us (94%)
  local copies, waits for them, and re-layouts  4.52 us (5%)
    pallas_call x1, Pallas kernels, local(): pl.pallas_call(functools.partial(kernel, n_band, n_sub, group), out_shape...  80.9 us
    unnamed x2, local copies, waits for them, and re-layouts  4.52 us

commit v1 on v0

--- a/solution.py
+++ b/solution.py
@@ -105,7 +105,8 @@
 def kernel(
     n_band, n_sub, group,
     ls_ref, vel_ref, nb_ref, adv_out, out_ref,
-    p0, pc, adv, sgn, vel, az, ay, halo, faces, local_m, pack_x, pack_y, unpack_x, unpack_y, tri, pres,
+    p0, pc, adv, sgn, vel, vz, az, ay, halo_x, halo_y, halo_z, faces_x, faces_y, faces_z,
+    local_m, pack_x, pack_y, unpack_x, unpack_y, tri, pres,
     nb_s, ids_s, krow, kcol, send_x, send_y, recv_x, recv_y, ar_send, ar_sub, ar_grp, ar_z, step_s,
     in_sem, out_sem, tx_sem, rx_sem, ar_tx, ar_rx,
 ):
@@ -182,27 +183,31 @@
         kcol[c * LANES : (c + 1) * LANES, :] = krow[:, c * LANES : (c + 1) * LANES].T
 
     def count(k, carry):
-        rows = pl.ds(pl.multiple_of(8 * k, 8), 8)
-        return tuple(
-            total + jnp.where(kcol[rows, d : d + 1] < krow[d : d + 1, :], 1.0, 0.0) for d, total in enumerate(carry)
-        )
+        for j in range(8):
+            rows = pl.ds(pl.multiple_of(64 * k + 8 * j, 8), 8)
+            carry = tuple(
+                total + jnp.where(kcol[rows, d : d + 1] < krow[d : d + 1, :], 1.0, 0.0)
+                for d, total in enumerate(carry)
+            )
+        return carry
 
     zero = jnp.zeros((8, TILES_DEV), F32)
-    counts = lax.fori_loop(0, TILES_DEV // 8, count, (zero,) * 4)
+    counts = lax.fori_loop(0, TILES_DEV // 64, count, (zero,) * 4)
     for d in range(4):
         rank = jnp.sum(counts[d], axis=0, keepdims=True).astype(jnp.int32)
         ids_s[1, d : d + 1, :] = jnp.where(remote[d : d + 1], rank, -1)
 
     def fill_pack(k, carry):
-        rows = pl.ds(pl.multiple_of(16 * k, 16), 16)
         lane_x = lax.broadcasted_iota(jnp.int32, (16, SLOTS_X), 1).astype(F32)
         lane_y = lax.broadcasted_iota(jnp.int32, (16, SLOTS_Y), 1).astype(F32)
-        for d in range(2):
-            pack_x[d, rows, :] = jnp.where(kcol[rows, 4 + d : 5 + d] == lane_x, 1.0, 0.0).astype(BF16)
-            pack_y[d, rows, :] = jnp.where(kcol[rows, 6 + d : 7 + d] == lane_y, 1.0, 0.0).astype(BF16)
+        for j in range(4):
+            rows = pl.ds(pl.multiple_of(64 * k + 16 * j, 16), 16)
+            for d in range(2):
+                pack_x[d, rows, :] = jnp.where(kcol[rows, 4 + d : 5 + d] == lane_x, 1.0, 0.0).astype(BF16)
+                pack_y[d, rows, :] = jnp.where(kcol[rows, 6 + d : 7 + d] == lane_y, 1.0, 0.0).astype(BF16)
         return carry
 
-    lax.fori_loop(0, TILES_DEV // 16, fill_pack, 0)
+    lax.fori_loop(0, TILES_DEV // 64, fill_pack, 0)
 
     def fill_unpack(d, dest):
         def body(k, carry):
@@ -219,12 +224,39 @@
     for copy in in_copies[:GROUPS]:
         copy.wait()
 
-    def copy_in(x, carry):
-        for g in range(GROUPS):
-            pc[g, x] = p0[g, x]
+    def put_face(ref, d, row, g, hi, lo):
+        col = pl.ds(pl.multiple_of(g * LANES, LANES), LANES)
+        ref[d, pl.ds(row, 16), col] = hi
+        ref[d, pl.ds(row + FACE, 16), col] = lo
+
+    def put_faces_xy(g, r, values):
+        parts = []
+        for x in range(8):
+            hi = values[x].astype(BF16)
+            rest = values[x] - hi.astype(F32)
+            parts.append(rest)
+            if x not in (3, 4):
+                put_face(faces_x, 0 if x > 4 else 1, 64 * (x - 5 if x > 4 else x) + 16 * r, g, hi, rest.astype(BF16))
+        for j in range(2):
+            y = 2 * r + j
+            if y in (3, 4):
+                continue
+            for i in range(4):
+                hi, lo = [
+                    jnp.concatenate([part[2 * i + e][8 * j : 8 * j + 8] for e in range(2)], axis=0).astype(BF16)
+                    for part in (values, parts)
+                ]
+                put_face(faces_y, 0 if y > 4 else 1, 64 * (y - 5 if y > 4 else y) + 16 * i, g, hi, lo)
+
+    def copy_in(g, carry):
+        for r in range(4):
+            values = [p0[g, x, 16 * r : 16 * r + 16, :] for x in range(8)]
+            for x in range(8):
+                pc[g, x, 16 * r : 16 * r + 16, :] = values[x]
+            put_faces_xy(g, r, values)
         return carry
 
-    lax.fori_loop(0, 8, copy_in, 0)
+    lax.fori_loop(0, GROUPS, copy_in, 0)
     for copy in in_copies[GROUPS:]:
         copy.wait()
 
@@ -236,17 +268,10 @@
             top = jnp.maximum(top, total)
         turned = [vel[2, g, x, pl.ds(z, 8, stride=8), :] for z in range(8)]
         for z in range(8):
-            az[g, x, 8 * z : 8 * z + 8, :] = turned[z]
+            vz[g, x, 8 * z : 8 * z + 8, :] = turned[z]
         return top
 
     top = lax.fori_loop(0, GROUPS * 8, speeds, jnp.zeros((8, LANES), F32))
-
-    def turn_back(idx, carry):
-        g, x = idx // 8, lax.rem(idx, 8)
-        vel[2, g, x] = az[g, x]
-        return carry
-
-    lax.fori_loop(0, GROUPS * 8, turn_back, 0)
 
     pl.semaphore_wait(barrier, len(peers))
 
@@ -297,143 +322,120 @@
             )
         return copies
 
-    def put_face(d, row, g, value):
-        hi, lo = split_rows(value)
-        col = pl.ds(pl.multiple_of(g * LANES, LANES), LANES)
-        faces[d, pl.ds(pl.multiple_of(row, 16), 16), col] = hi
-        faces[d, pl.ds(pl.multiple_of(row + FACE, 16), 16), col] = lo
-
-    def faces_x():
-        def body(idx, carry):
-            g, r = idx // 4, lax.rem(idx, 4)
-            rows = pl.ds(pl.multiple_of(16 * r, 16), 16)
-            for d, start in ((0, 5), (1, 0)):
-                for l in range(3):
-                    put_face(d, 64 * l + 16 * r, g, pc[g, start + l, rows, :])
-            return carry
-
-        lax.fori_loop(0, 4 * GROUPS, body, 0)
-
-    def faces_y():
-        def body(idx, carry):
-            g, i = idx // 4, lax.rem(idx, 4)
-            for d, start in ((2, 5), (3, 0)):
-                for l in range(3):
-                    y = start + l
-                    value = pc[g, pl.ds(2 * i, 2), 8 * y : 8 * y + 8, :].reshape(16, LANES)
-                    put_face(d, 64 * l + 16 * i, g, value)
-            return carry
-
-        lax.fori_loop(0, 4 * GROUPS, body, 0)
-
     def turned_pair(ref, g, i, k):
         return jnp.concatenate([ref[g, 2 * i + j, pl.ds(k, 8, stride=8), :] for j in range(2)], axis=0)
 
-    def faces_z():
-        def body(idx, carry):
-            g, i = idx // 4, lax.rem(idx, 4)
-            for d, start in ((4, 5), (5, 0)):
-                for l in range(3):
-                    put_face(d, 64 * l + 16 * i, g, turned_pair(pc, g, i, start + l))
-            return carry
-
-        lax.fori_loop(0, 4 * GROUPS, body, 0)
+    def put_faces_z():
+        for g in range(GROUPS):
+            for i in range(4):
+                for d, start in ((0, 5), (1, 0)):
+                    for l in range(3):
+                        hi, lo = split_rows(turned_pair(pc, g, i, start + l))
+                        put_face(faces_z, d, 64 * l + 16 * i, g, hi, lo)
 
     def two_part_dot(lhs, rhs):
         res = jnp.dot(lhs, rhs, preferred_element_type=F32)
         return res[:FACE] + res[FACE:]
 
-    def gather(d):
-        res = two_part_dot(faces[d], local_m[d])
+    def gather(faces, d, matrix, halo):
+        res = two_part_dot(faces[d], matrix)
         for g in range(GROUPS):
             halo[d, g] = res[:, g * LANES : (g + 1) * LANES]
 
-    def unpack(d, t):
-        block = recv_x[t, d] if d < 2 else recv_y[t, d - 2]
+    def unpack(block, d, matrix, halo):
         hi, lo = split_rows(block)
-        matrix = unpack_x[d] if d < 2 else unpack_y[d - 2]
         res = two_part_dot(jnp.concatenate([hi, lo], axis=0), matrix)
         for g in range(GROUPS):
             halo[d, g] = halo[d, g] + res[:, g * LANES : (g + 1) * LANES]
 
-    def padded(d, g, row, cells):
-        rows = [pl.ds(pl.multiple_of(64 * l + row, 16), 16) for l in range(3)]
-        there_lo = pres[d, g] > 0
-        there_hi = pres[d + 1, g] > 0
-        low = [jnp.where(there_lo, halo[d, g, rows[l], :], cells[0]) for l in range(3)]
-        high = [jnp.where(there_hi, halo[d + 1, g, rows[l], :], cells[7]) for l in range(3)]
+    def padded(halo, there, g, row, cells):
+        there_lo = pres[there, g] > 0
+        there_hi = pres[there + 1, g] > 0
+        low = [jnp.where(there_lo, halo[0, g, pl.ds(64 * l + row, 16), :], cells[0]) for l in range(3)]
+        high = [jnp.where(there_hi, halo[1, g, pl.ds(64 * l + row, 16), :], cells[7]) for l in range(3)]
         return low + cells + high
 
     def pair(ref, g, i, k):
-        return ref[g, pl.ds(2 * i, 2), 8 * k : 8 * k + 8, :].reshape(16, LANES)
-
-    def z_lines(line, extra, g, i):
-        cells = [turned_pair(pc, g, i, z) for z in range(8)]
-        for z, value in enumerate(line(padded(4, g, 16 * i, cells), extra(g, i))):
-            az[g, pl.ds(2 * i, 2), 8 * z : 8 * z + 8, :] = value.reshape(2, 8, LANES)
-
-    def y_lines(line, extra, g, i):
-        cells = [pair(pc, g, i, y) for y in range(8)]
-        for y, value in enumerate(line(padded(2, g, 16 * i, cells), extra(g, i))):
-            ay[g, pl.ds(2 * i, 2), 8 * y : 8 * y + 8, :] = (value + turned_pair(az, g, i, y)).reshape(2, 8, LANES)
-
-    def x_lines(line, extra, finish, g, r):
-        rows = pl.ds(pl.multiple_of(16 * r, 16), 16)
-        cells = [pc[g, x, rows, :] for x in range(8)]
-        for x, value in enumerate(line(padded(0, g, 16 * r, cells), extra(g, rows))):
-            finish(g, x, rows, cells[x], value + ay[g, x, rows, :])
-
-    def begin(t):
-        faces_x()
+        return ref[g, 2 * i : 2 * i + 2, 8 * k : 8 * k + 8, :].reshape(16, LANES)
+
+    def z_lines(line, extra, g):
+        for i in range(4):
+            cells = [turned_pair(pc, g, i, z) for z in range(8)]
+            values = line(padded(halo_z, 4, g, 16 * i, cells), [extra(g, i, z) for z in range(8)])
+            for z in range(8):
+                az[g, 2 * i : 2 * i + 2, 8 * z : 8 * z + 8, :] = values[z].reshape(2, 8, LANES)
+
+    def y_lines(line, extra, g):
+        for i in range(4):
+            cells = [pair(pc, g, i, y) for y in range(8)]
+            values = line(padded(halo_y, 2, g, 16 * i, cells), [extra(g, i, y) for y in range(8)])
+            for y in range(8):
+                total = values[y] + turned_pair(az, g, i, y)
+                ay[g, 2 * i : 2 * i + 2, 8 * y : 8 * y + 8, :] = total.reshape(2, 8, LANES)
+
+    def x_lines(line, extra, finish, g):
+        for r in range(4):
+            rows = slice(16 * r, 16 * r + 16)
+            cells = [pc[g, x, rows, :] for x in range(8)]
+            values = line(padded(halo_x, 0, g, 16 * r, cells), [extra(g, x, rows) for x in range(8)])
+            fresh = [finish(g, x, rows, cells[x], values[x] + ay[g, x, rows, :]) for x in range(8)]
+            put_faces_xy(g, r, fresh)
+
+    def run(t, line, extra_z, extra_y, extra_x, finish, after_z=None, after_y=None):
         copies = exchange(t)
-        send_x[0] = two_part_dot(faces[1], pack_x[0])
+        send_x[0] = two_part_dot(faces_x[1], pack_x[0])
         copies[0].start()
-        send_x[1] = two_part_dot(faces[0], pack_x[1])
+        send_x[1] = two_part_dot(faces_x[0], pack_x[1])
         copies[1].start()
-        faces_y()
-        send_y[0] = two_part_dot(faces[3], pack_y[0])
+        send_y[0] = two_part_dot(faces_y[1], pack_y[0])
         copies[2].start()
-        send_y[1] = two_part_dot(faces[2], pack_y[1])
+        send_y[1] = two_part_dot(faces_y[0], pack_y[1])
         copies[3].start()
-        faces_z()
-        gather(4)
-        gather(5)
-        return copies
-
-    def run(t, line, extra_z, extra_y, extra_x, finish, after_z=None, after_y=None):
-        copies = begin(t)
-
-        def z_body(k, carry):
-            gather(k)
-            for i in range(4):
-                z_lines(line, extra_z, k, i)
+        put_faces_z()
+        gather(faces_z, 0, local_m[4], halo_z)
+        gather(faces_z, 1, local_m[5], halo_z)
+
+        def z_first(k, carry):
+            gather(faces_y, k, local_m[2 + k], halo_y)
+            z_lines(line, extra_z, k)
             return carry
 
-        lax.fori_loop(0, 4, z_body, 0)
+        lax.fori_loop(0, 2, z_first, 0)
+        copies[2].wait_recv()
+        copies[3].wait_recv()
+
+        def z_second(k, carry):
+            gather(faces_x, k, local_m[k], halo_x)
+            unpack(recv_y[t, k], k, unpack_y[k], halo_y)
+            z_lines(line, extra_z, 2 + k)
+            return carry
+
+        lax.fori_loop(0, 2, z_second, 0)
         if after_z is not None:
             after_z()
-        copies[2].wait_recv()
-        copies[3].wait_recv()
-        unpack(2, t)
-        unpack(3, t)
-
-        def y_body(k, carry):
-            y_lines(line, extra_y, k // 4, lax.rem(k, 4))
+
+        def y_first(k, carry):
+            y_lines(line, extra_y, k)
             return carry
 
-        lax.fori_loop(0, 4 * GROUPS, y_body, 0)
+        lax.fori_loop(0, 2, y_first, 0)
+        copies[0].wait_recv()
+        copies[1].wait_recv()
+
+        def y_second(k, carry):
+            unpack(recv_x[t, k], k, unpack_x[k], halo_x)
+            y_lines(line, extra_y, 2 + k)
+            return carry
+
+        lax.fori_loop(0, 2, y_second, 0)
         if after_y is not None:
             after_y()
-        copies[0].wait_recv()
-        copies[1].wait_recv()
-        unpack(0, t)
-        unpack(1, t)
-
-        def x_body(k, carry):
-            x_lines(line, extra_x, finish, k // 4, lax.rem(k, 4))
+
+        def x_all(k, carry):
+            x_lines(line, extra_x, finish, k)
             return carry
 
-        lax.fori_loop(0, 4 * GROUPS, x_body, 0)
+        lax.fori_loop(0, GROUPS, x_all, 0)
         for copy in copies:
             copy.wait_send()
 
@@ -459,13 +461,14 @@
             pc[g, x, rows, :] = value
             adv[g, x, rows, :] = value
             sgn[g, x, rows, :] = jnp.where(value > 0, 1.0, -1.0)
+            return value
 
         run(
             t,
             advect_line,
-            lambda g, i: [pair(vel.at[2], g, i, z) for z in range(8)],
-            lambda g, i: [pair(vel.at[1], g, i, y) for y in range(8)],
-            lambda g, rows: [vel[0, g, x, rows, :] for x in range(8)],
+            lambda g, i, z: pair(vz, g, i, z),
+            lambda g, i, y: pair(vel.at[1], g, i, y),
+            lambda g, x, rows: vel[0, g, x, rows, :],
             finish,
             after_z,
             after_y,
@@ -485,14 +488,16 @@
             v = adv[g, x, rows, :]
             sign = v * lax.rsqrt(v * v + 1.0)
             root = total * (1.0 / 36.0) + ROOT_EPS
-            pc[g, x, rows, :] = cell + (DTAU * sign) * (1.0 - root * lax.rsqrt(root))
+            value = cell + (DTAU * sign) * (1.0 - root * lax.rsqrt(root))
+            pc[g, x, rows, :] = value
+            return value
 
         run(
             STAGES + k,
             reinit_line,
-            lambda g, i: [turned_pair(sgn, g, i, z) for z in range(8)],
-            lambda g, i: [pair(sgn, g, i, y) for y in range(8)],
-            lambda g, rows: [sgn[g, x, rows, :] for x in range(8)],
+            lambda g, i, z: turned_pair(sgn, g, i, z),
+            lambda g, i, y: pair(sgn, g, i, y),
+            lambda g, x, rows: sgn[g, x, rows, :],
             finish,
         )
         return carry
@@ -505,6 +510,22 @@
     for copy in out_copies:
         copy.start()
     for copy in adv_copies + out_copies:
+        copy.wait()
+
+
+def hand_over(a_ref, b_ref, x_ref, y_ref, buf, sem):
+    ins, outs = [], []
+    for k in range(4):
+        part = pl.ds(2 * k, 2)
+        for i, (src, dst) in enumerate(((a_ref, x_ref), (b_ref, y_ref))):
+            ins.append(pltpu.make_async_copy(src.at[part], buf.at[i, part], sem.at[0, 2 * k + i]))
+            outs.append(pltpu.make_async_copy(buf.at[i, part], dst.at[part], sem.at[1, 2 * k + i]))
+    for copy in ins:
+        copy.start()
+    for arrived, onward in zip(ins, outs):
+        arrived.wait()
+        onward.start()
+    for copy in outs:
         copy.wait()
 
 
@@ -530,8 +551,13 @@
                 pltpu.VMEM((3,) + cells, F32),
                 pltpu.VMEM(cells, F32),
                 pltpu.VMEM(cells, F32),
-                pltpu.VMEM((6, GROUPS, FACE, LANES), F32),
-                pltpu.VMEM((6, 2 * FACE, TILES_DEV), BF16),
+                pltpu.VMEM(cells, F32),
+                pltpu.VMEM((2, GROUPS, FACE, LANES), F32),
+                pltpu.VMEM((2, GROUPS, FACE, LANES), F32),
+                pltpu.VMEM((2, GROUPS, FACE, LANES), F32),
+                pltpu.VMEM((2, 2 * FACE, TILES_DEV), BF16),
+                pltpu.VMEM((2, 2 * FACE, TILES_DEV), BF16),
+                pltpu.VMEM((2, 2 * FACE, TILES_DEV), BF16),
                 pltpu.VMEM((6, TILES_DEV, TILES_DEV), BF16),
                 pltpu.VMEM((2, TILES_DEV, SLOTS_X), BF16),
                 pltpu.VMEM((2, TILES_DEV, SLOTS_Y), BF16),
@@ -563,6 +589,13 @@
                 collective_id=0, has_side_effects=True, vmem_limit_bytes=56 * 2**20
             ),
         )(level_set.reshape(8, 64, TILES_DEV), velocity.reshape(3, 8, 64, TILES_DEV), neighbours)
+        advected, reinitialized = pl.pallas_call(
+            hand_over,
+            out_shape=(whole, whole),
+            in_specs=[anywhere, anywhere],
+            out_specs=(anywhere, anywhere),
+            scratch_shapes=[pltpu.VMEM((2, 8, 64, TILES_DEV), F32), pltpu.SemaphoreType.DMA((2, 8))],
+        )(advected, reinitialized)
         return advected.reshape(8, 8, 8, TILES_DEV), reinitialized.reshape(8, 8, 8, TILES_DEV)
 
     return jax.shard_map(

time: 86.3 us -> 80.3 us (0.930)
  local copies, waits for them, and re-layouts: 4.52 us -> 0 us
  Pallas kernels: 80.9 us -> 79.4 us
    unnamed x2 -> x0, local copies, waits for them, and re-layouts: 4.52 us -> none
    pallas_call x1, Pallas kernels: 80.9 us -> 77 us  [local(): pl.pallas_call(functools.partial(kernel, n_band, n_sub, group), out_shape...]
    pallas_call x0 -> x1, Pallas kernels: none -> 2.4 us  [local(): pl.pallas_call(hand_over, out_shape=(whole, whole), in_specs=[anywhere, a...]
where the time goes in v1:
time: 80.3 us; the launch traced here: 80.1 us
  Pallas kernels  79.4 us (99%)
    pallas_call x1, Pallas kernels, local(): pl.pallas_call(functools.partial(kernel, n_band, n_sub, group), out_shape...  77 us
    pallas_call x1, Pallas kernels, local(): pl.pallas_call(hand_over, out_shape=(whole, whole), in_specs=[anywhere, a...  2.4 us

profile of v1, /device:TPU:0, one launch (start us, length us, event | category | flops | bytes accessed | tf_op | source)
XLA Modules:
  0.0 80.1 jit_solution(3769896408983421845)
XLA Ops:
  0.6 77.0 %shard_map.50 = (f32[8,64,512]{2,1,0:T(8,128)}, f32[8,64,512]{2,1,0:T(8,128)}) custom-call(f32[8,64,512]{2,1,0:T(8,128)} %bitcast.5, f32[3,8,64,512]{3,2,1,0:T(8,128)} %bitcast.4, s32[6,512]{1,0:T(8,128)} %nb_ref.1), custom_call_target="tpu_custom_call" | custom-call | tf_op jit(solution)/shard_map/pallas_call | solution.py:541
  77.7 2.4 %shard_map.51 = (f32[8,64,512]{2,1,0:T(8,128)}, f32[8,64,512]{2,1,0:T(8,128)}) custom-call(f32[8,64,512]{2,1,0:T(8,128)} %get-tuple-element.6.a_ref, f32[8,64,512]{2,1,0:T(8,128)} %get-tuple-element.7.b_ref), custom_call_target="tpu_custom_call" | custom-call | tf_op jit(solution)/shard_map/pallas_call | solution.py:592

commit v2 on v1

v2 whole, which is shorter than its diff:
```python
import functools

import jax
import jax.numpy as jnp
from jax import lax
from jax.experimental import pallas as pl
from jax.experimental.pallas import tpu as pltpu
from jax.sharding import PartitionSpec as P

TILES_DEV = 512
SLOTS_X = 256
SLOTS_Y = 32
BLOCK = 48
STAGES = 3
REINIT = 2
STEPS = STAGES + REINIT
EPS = 1e-06
CFL = 0.5
DTAU = 0.3
ROOT_EPS = 1e-06
LANES = 128
GROUPS = TILES_DEV // LANES

F32 = jnp.float32
BF16 = jnp.bfloat16
MESH = pl.DeviceIdType.MESH


def differences(p):
    first = [p[k + 1] - p[k] for k in range(13)]
    second = [first[k + 1] - first[k] for k in range(12)]
    third = [second[k + 1] - second[k] for k in range(11)]
    fourth = [None] + [third[k] - third[k - 1] for k in range(1, 11)]
    square = [e * e for e in second]
    ind_a, ind_b, ind_c = {}, {}, {}
    for k in range(11):
        half = (0.5 * second[k]) * second[k + 1]
        base = third[k] * third[k] * (2.0 / 3.0) + 0.5 * EPS
        low = base - half
        if k <= 8:
            ind_a[k] = low + square[k + 1]
        if 1 <= k <= 9:
            ind_b[k] = base + half
        if k >= 2:
            ind_c[k] = low + square[k]
    return third, fourth, ind_a, ind_b, ind_c


def recip(x):
    return pl.reciprocal(x, approx=True)


def advect_line(p, flow):
    third, fourth, ind_a, ind_b, ind_c = differences(p)
    out = []
    for c in range(8):
        up = flow[c] > 0
        ra = recip(jnp.where(up, ind_a[c], ind_c[c + 3]))
        rb = recip(jnp.where(up, ind_b[c + 1], ind_b[c + 2]))
        rc = recip(jnp.where(up, ind_c[c + 2], ind_a[c + 1]))
        wa = ra * ra
        wb = rb * rb * 6.0
        wc = rc * rc * 3.0
        far = jnp.where(up, fourth[c + 1], fourth[c + 3])
        num = wa * (far + far) + wc * fourth[c + 2]
        corr = num * recip(wa + wb + wc)
        linear = 3.0 * (p[c + 4] - p[c + 2]) - jnp.where(up, third[c + 1], third[c + 2])
        out.append(flow[c] * linear - jnp.abs(flow[c]) * corr)
    return out


def reinit_line(p, sign):
    third, fourth, ind_a, ind_b, ind_c = differences(p)
    wa, wa3, wb, wc, wc3 = {}, {}, {}, {}, {}
    for k, v in ind_a.items():
        r = recip(v)
        wa[k] = r * r
        wa3[k] = wa[k] * 3.0
    for k, v in ind_b.items():
        r = recip(v)
        wb[k] = r * r * 6.0
    for k, v in ind_c.items():
        r = recip(v)
        wc[k] = r * r
        wc3[k] = wc[k] * 3.0
    twice = [None] + [f + f for f in fourth[1:]]
    out = []
    for c in range(8):
        linear = 3.0 * (p[c + 4] - p[c + 2])
        corr_b = (wa[c] * twice[c + 1] + wc3[c + 2] * fourth[c + 2]) * recip(wa[c] + wb[c + 1] + wc3[c + 2])
        corr_f = (wc[c + 3] * twice[c + 3] + wa3[c + 1] * fourth[c + 2]) * recip(wc[c + 3] + wb[c + 2] + wa3[c + 1])
        back = linear - third[c + 1] - corr_b
        fore = third[c + 2] - linear - corr_f
        m = jnp.maximum(jnp.maximum(sign[c] * back, sign[c] * fore), 0.0)
        out.append(m * m)
    return out


def split_rows(value):
    hi = value.astype(BF16)
    lo = (value - hi.astype(F32)).astype(BF16)
    return jnp.concatenate([hi, lo], axis=0)


def two_part_dot(lhs, rhs):
    res = jnp.dot(lhs, rhs, preferred_element_type=F32)
    blocks = res.shape[0] // (2 * BLOCK)
    return [
        res[2 * BLOCK * k : 2 * BLOCK * k + BLOCK] + res[2 * BLOCK * k + BLOCK : 2 * BLOCK * (k + 1)]
        for k in range(blocks)
    ]


def kernel(
    n_band, n_sub, low,
    ls_ref, vel_ref, nb_ref, adv_out, out_ref,
    p0, pc, adv, sgn, vel, vz, az, ay,
    local_x, local_y, halo_xa, halo_xb, halo_ya, halo_yb, halo_za, halo_zb, faces_xa, faces_xb, faces_y,
    local_m, pack_x, pack_y, unpack_x, unpack_y, tri, pres,
    nb_s, ids_s, krow, kcol, send_x, send_y, recv_x, recv_y, ar_send, ar_near, ar_far, step_s,
    in_sem, out_sem, tx_x, rx_x, tx_y, rx_y, ar_tx, ar_rx,
):
    band = lax.axis_index("band")
    sub = lax.axis_index("sub")
    n_high = n_band // low
    n_near = low * n_sub
    band_up, band_dn = lax.rem(band + 1, n_band), lax.rem(band + n_band - 1, n_band)
    sub_up, sub_dn = lax.rem(sub + 1, n_sub), lax.rem(sub + n_sub - 1, n_sub)
    band_low = lax.rem(band, low)

    def near_peer(d):
        return (band - band_low + lax.rem(band_low + d // n_sub, low), lax.rem(sub + d % n_sub, n_sub))

    def far_peer(d):
        return (lax.rem(band + d * low, n_band), sub)

    def lanes(g):
        return pl.ds(g * LANES, LANES)

    in_copies = []
    for k in range(3):
        for g in range(GROUPS):
            in_copies.append(
                pltpu.make_async_copy(vel_ref.at[k, :, :, lanes(g)], vel.at[k, g], in_sem.at[4 * k + g])
            )
    for g in range(GROUPS):
        in_copies.append(pltpu.make_async_copy(ls_ref.at[:, :, lanes(g)], p0.at[g], in_sem.at[12 + g]))
    for copy in in_copies:
        copy.start()

    peers = [(band_up, sub), (band_dn, sub)]
    peers += [near_peer(d) for d in range(1, n_near)]
    peers += [far_peer(d) for d in range(1, n_high)]
    barrier = pltpu.get_barrier_semaphore()
    for peer in peers:
        pl.semaphore_signal(barrier, inc=1, device_id=peer, device_id_type=MESH)

    nb_s[...] = jnp.full((8, TILES_DEV), -1, jnp.int32)
    nb_s[0:6, :] = nb_ref[...]
    nb = nb_s[...]
    base = (band * n_sub + sub) * TILES_DEV
    present = nb >= 0
    is_local = (nb >= base) & (nb < base + TILES_DEV)
    remote = present & jnp.logical_not(is_local)
    ids_s[0] = jnp.where(is_local, nb - base, -1)
    presf = jnp.where(present, 1.0, 0.0)
    for d in range(6):
        for g in range(GROUPS):
            pres[d, g] = jnp.broadcast_to(presf[d : d + 1, g * LANES : (g + 1) * LANES], (16, LANES))

    def fill_tri(k, carry):
        rows = pl.ds(pl.multiple_of(16 * k, 16), 16)
        iota = lax.broadcasted_iota(jnp.int32, (16, TILES_DEV), 0) + 16 * k
        lane = lax.broadcasted_iota(jnp.int32, (16, TILES_DEV), 1)
        tri[rows, :] = jnp.where(iota < lane, 1.0, 0.0).astype(BF16)
        return carry

    lax.fori_loop(0, TILES_DEV // 16, fill_tri, 0)
    flags = jnp.where(remote, 1.0, 0.0)
    flags16 = jnp.concatenate([flags, jnp.zeros_like(flags)], axis=0).astype(BF16)
    place = jnp.dot(flags16, tri[...], preferred_element_type=F32)[0:8]
    keys = jnp.where(remote, nb.astype(F32), 1e9)
    krow[...] = jnp.zeros_like(krow)
    krow[0:4, :] = keys[0:4]
    krow[4:8, :] = jnp.where(remote, place, -1.0)[0:4]
    for c in range(GROUPS):
        kcol[c * LANES : (c + 1) * LANES, :] = krow[:, c * LANES : (c + 1) * LANES].T

    for copy in in_copies[: 3 * GROUPS]:
        copy.wait()

    def speeds(idx, top):
        g, x = idx // 8, lax.rem(idx, 8)
        for y in range(8):
            rows = slice(8 * y, 8 * y + 8)
            total = jnp.abs(vel[0, g, x, rows, :]) + jnp.abs(vel[1, g, x, rows, :]) + jnp.abs(vel[2, g, x, rows, :])
            top = jnp.maximum(top, total)
        for z in range(8):
            vz[g, x, 8 * z : 8 * z + 8, :] = vel[2, g, x, pl.ds(z, 8, stride=8), :]
        return top

    top = lax.fori_loop(0, GROUPS * 8, speeds, jnp.zeros((8, LANES), F32))

    pl.semaphore_wait(barrier, len(peers))

    def ar_copies(r):
        peer, slots, n = ((near_peer, ar_near, n_near), (far_peer, ar_far, n_high))[r]
        first = (0, n_near)[r]
        return [
            pltpu.make_async_remote_copy(
                src_ref=ar_send.at[r],
                dst_ref=slots.at[d - 1],
                send_sem=ar_tx.at[first + d - 1],
                recv_sem=ar_rx.at[first + d - 1],
                device_id=peer(d),
                device_id_type=MESH,
            )
            for d in range(1, n)
        ], slots

    def ar_start(r, value):
        ar_send[r] = value
        for copy in ar_copies(r)[0]:
            copy.start()

    def ar_finish(r):
        value = ar_send[r]
        copies, slots = ar_copies(r)
        for k, copy in enumerate(copies):
            copy.wait()
            value = jnp.maximum(value, slots[k])
        return value

    ar_start(0, top)

    def copy_x(t, d, r):
        return pltpu.make_async_remote_copy(
            src_ref=send_x.at[d, r],
            dst_ref=recv_x.at[t, 1 - d, r],
            send_sem=tx_x.at[d, r],
            recv_sem=rx_x.at[t, d, r],
            device_id=((band_dn, sub), (band_up, sub))[d],
            device_id_type=MESH,
        )

    def copy_y(t, d):
        return pltpu.make_async_remote_copy(
            src_ref=send_y.at[d],
            dst_ref=recv_y.at[t, 1 - d],
            send_sem=tx_y.at[d],
            recv_sem=rx_y.at[t, d],
            device_id=((band, sub_dn), (band, sub_up))[d],
            device_id_type=MESH,
        )

    def fill_pack(k, carry):
        lane_x = lax.broadcasted_iota(jnp.int32, (16, SLOTS_X), 1).astype(F32)
        lane_y = lax.broadcasted_iota(jnp.int32, (16, LANES), 1).astype(F32)
        for j in range(4):
            rows = pl.ds(pl.multiple_of(64 * k + 16 * j, 16), 16)
            for d in range(2):
                pack_x[d, rows, :] = jnp.where(kcol[rows, 4 + d : 5 + d] == lane_x, 1.0, 0.0).astype(BF16)
                pack_y[d, rows, :] = jnp.where(kcol[rows, 6 + d : 7 + d] == lane_y, 1.0, 0.0).astype(BF16)
        return carry

    lax.fori_loop(0, TILES_DEV // 64, fill_pack, 0)

    def put_face(ref, lead, l, col, hi, lo):
        ref[(*lead, pl.ds(16 * l, 16), col)] = hi
        ref[(*lead, pl.ds(BLOCK + 16 * l, 16), col)] = lo

    def put_faces_xy(g, q, odd, values):
        col = pl.ds(g * LANES, LANES)
        parts = []
        for x in range(8):
            hi = values[x].astype(BF16)
            rest = values[x] - hi.astype(F32)
            parts.append(rest)
            if x not in (3, 4):
                put_face(faces_xb if odd else faces_xa, (0 if x > 4 else 1, q), x - 5 if x > 4 else x, col, hi, rest.astype(BF16))
        for j in range(2):
            for i in range(4):
                hi, lo = [
                    jnp.concatenate([part[2 * i + e][8 * j : 8 * j + 8] for e in range(2)], axis=0).astype(BF16)
                    for part in (values, parts)
                ]
                row = 2 * odd + j
                faces_y[q, i, pl.ds(16 * row, 16), col] = hi
                faces_y[q, i, pl.ds(64 + 16 * row, 16), col] = lo

    def pack_block_x(ref, q, r):
        for d in range(2):
            send_x[d, r] = two_part_dot(ref[1 - d, q], pack_x[d])[0]

    def copy_in(q, carry):
        for odd in range(2):
            for g in range(GROUPS):
                rows = pl.ds(pl.multiple_of(32 * q + 16 * odd, 16), 16)
                values = [p0[g, x, rows, :] for x in range(8)]
                for x in range(8):
                    pc[g, x, rows, :] = values[x]
                put_faces_xy(g, q, odd, values)
            pack_block_x(faces_xb if odd else faces_xa, q, 2 * q + odd)
            for d in range(2):
                copy_x(0, d, 2 * q + odd).start()
        return carry

    for copy in in_copies[3 * GROUPS :]:
        copy.wait()
    lax.fori_loop(0, 2, copy_in, 0)

    def fill(k, carry):
        for j in range(2):
            rows = pl.ds(pl.multiple_of(32 * k + 16 * j, 16), 16)
            iota = lax.broadcasted_iota(jnp.int32, (16, TILES_DEV), 0) + (32 * k + 16 * j)
            for d in range(6):
                local_m[d, rows, :] = jnp.where(iota == ids_s[0, d : d + 1, :], 1.0, 0.0).astype(BF16)
        return carry

    lax.fori_loop(0, TILES_DEV // 32, fill, 0)

    def count(k, carry):
        for j in range(8):
            rows = pl.ds(pl.multiple_of(64 * k + 8 * j, 8), 8)
            carry = tuple(
                total + jnp.where(kcol[rows, d : d + 1] < krow[d : d + 1, :], 1.0, 0.0)
                for d, total in enumerate(carry)
            )
        return carry

    zero = jnp.zeros((8, TILES_DEV), F32)
    counts = lax.fori_loop(0, TILES_DEV // 64, count, (zero,) * 4)
    for d in range(4):
        rank = jnp.sum(counts[d], axis=0, keepdims=True).astype(jnp.int32)
        ids_s[1, d : d + 1, :] = jnp.where(remote[d : d + 1], rank, -1)

    def fill_unpack(dest, first):
        def body(k, carry):
            for j in range(2):
                rows = pl.ds(pl.multiple_of(32 * k + 16 * j, 16), 16)
                iota = lax.broadcasted_iota(jnp.int32, (16, TILES_DEV), 0) + (32 * k + 16 * j)
                for d in range(2):
                    dest[d, rows, :] = jnp.where(iota == ids_s[1, first + d : first + d + 1, :], 1.0, 0.0).astype(BF16)
            return carry

        lax.fori_loop(0, dest.shape[1] // 32, body, 0)

    fill_unpack(unpack_x, 0)
    fill_unpack(unpack_y, 2)

    def turned_pair(ref, g, i, k):
        return jnp.concatenate([ref[g, 2 * i + j, pl.ds(k, 8, stride=8), :] for j in range(2)], axis=0)

    def pair(ref, g, i, k):
        return ref[g, pl.ds(2 * i, 2), 8 * k : 8 * k + 8, :].reshape(16, LANES)

    def face_y(d, i):
        first = 16 * (1 - d)
        return jnp.concatenate(
            [faces_y[1 - d, i, pl.ds(pl.multiple_of(64 * part + first, 16), BLOCK), :] for part in range(2)], axis=0
        )

    def put_halo(halo, d, res, local):
        for g in range(GROUPS):
            part = res[:, g * LANES : (g + 1) * LANES]
            halo[d, g] = part if local is None else part + local[g]

    def prepare_z(i, halo):
        for d, start in ((0, 5), (1, 0)):
            value = jnp.concatenate(
                [
                    jnp.concatenate([turned_pair(pc, g, i, start + l) for g in range(GROUPS)], axis=1)
                    for l in range(3)
                ],
                axis=0,
            )
            put_halo(halo, d, two_part_dot(split_rows(value), local_m[4 + d])[0], None)

    def prepare_y(t, i, halo):
        for d in range(2):
            block = pltpu.roll(recv_y[t, d], lax.rem((4 - i) * SLOTS_Y, LANES), 1)
            res = two_part_dot(split_rows(block), unpack_y[d])[0]
            put_halo(halo, d, res, [local_y[d, g, i] for g in range(GROUPS)])

    def prepare_x(t, r, q, odd, halo):
        for d in range(2):
            res = two_part_dot(split_rows(recv_x[t, d, r]), unpack_x[d])[0]
            put_halo(halo, d, res, [local_x[d, g, odd, q] for g in range(GROUPS)])

    def gather_y(d):
        faces = jnp.concatenate([face_y(d, i) for i in range(4)], axis=0)
        for i, res in enumerate(two_part_dot(faces, local_m[2 + d])):
            for g in range(GROUPS):
                local_y[d, g, i] = res[:, g * LANES : (g + 1) * LANES]

    def gather_x(d):
        faces = jnp.concatenate([ref[d, q] for ref in (faces_xa, faces_xb) for q in range(2)], axis=0)
        for k, res in enumerate(two_part_dot(faces, local_m[d])):
            for g in range(GROUPS):
                local_x[d, g, k // 2, k % 2] = res[:, g * LANES : (g + 1) * LANES]

    def padded(halo, there, g, cells):
        there_lo = pres[there, g] > 0
        there_hi = pres[there + 1, g] > 0
        before = [jnp.where(there_lo, halo[0, g, 16 * l : 16 * l + 16, :], cells[0]) for l in range(3)]
        after = [jnp.where(there_hi, halo[1, g, 16 * l : 16 * l + 16, :], cells[7]) for l in range(3)]
        return before + cells + after

    def z_lines(line, extra, i, halo):
        for g in range(GROUPS):
            cells = [turned_pair(pc, g, i, z) for z in range(8)]
            values = line(padded(halo, 4, g, cells), [extra(g, i, z) for z in range(8)])
            for z in range(8):
                az[g, pl.ds(2 * i, 2), 8 * z : 8 * z + 8, :] = values[z].reshape(2, 8, LANES)

    def y_lines(line, extra, i, halo):
        for g in range(GROUPS):
            cells = [pair(pc, g, i, y) for y in range(8)]
            values = line(padded(halo, 2, g, cells), [extra(g, i, y) for y in range(8)])
            for y in range(8):
                total = values[y] + turned_pair(az, g, i, y)
                ay[g, pl.ds(2 * i, 2), 8 * y : 8 * y + 8, :] = total.reshape(2, 8, LANES)

    def x_lines(line, extra, finish, q, odd, halo):
        rows = pl.ds(pl.multiple_of(32 * q + 16 * odd, 16), 16)
        ahead = [pc[0, x, rows, :] for x in range(8)]
        for g in range(GROUPS):
            cells = ahead
            if g + 1 < GROUPS:
                ahead = [pc[g + 1, x, rows, :] for x in range(8)]
            values = line(padded(halo, 0, g, cells), [extra(g, x, rows) for x in range(8)])
            fresh = [finish(g, x, rows, cells[x], values[x] + ay[g, x, rows, :]) for x in range(8)]
            put_faces_xy(g, q, odd, fresh)

    def run(t, line, extra_z, extra_y, extra_x, finish, after_z=None, after_y=None):
        for d in range(2):
            parts = [two_part_dot(face_y(1 - d, i), pack_y[d])[0] for i in range(4)]
            send_y[d] = sum(pltpu.roll(parts[i], i * SLOTS_Y, 1) if i else parts[i] for i in range(4))
            copy_y(t, d).start()
        prepare_z(0, halo_za)

        def z_body(q, carry):
            prepare_z(2 * q + 1, halo_zb)
            gather_y(q)
            z_lines(line, extra_z, 2 * q, halo_za)
            prepare_z(lax.rem(2 * q + 2, 4), halo_za)
            z_lines(line, extra_z, 2 * q + 1, halo_zb)
            return carry

        lax.fori_loop(0, 2, z_body, 0)
        if after_z is not None:
            after_z()
        for d in range(2):
            copy_y(t, d).wait()
        prepare_y(t, 0, halo_ya)

        def y_body(q, carry):
            prepare_y(t, 2 * q + 1, halo_yb)
            gather_x(q)
            y_lines(line, extra_y, 2 * q, halo_ya)
            prepare_y(t, lax.rem(2 * q + 2, 4), halo_ya)
            y_lines(line, extra_y, 2 * q + 1, halo_yb)
            return carry

        lax.fori_loop(0, 2, y_body, 0)
        if after_y is not None:
            after_y()

        def wait_x(r):
            for d in range(2):
                copy_x(t, d, r).wait_recv()

        for r in range(4):
            for d in range(2):
                copy_x(t, d, r).wait_send()
        wait_x(0)
        prepare_x(t, 0, 0, 0, halo_xa)

        def x_body(q, carry):
            wait_x(2 * q + 1)
            prepare_x(t, 2 * q + 1, q, 1, halo_xb)
            pack_block_x(faces_xb, lax.rem(q + 1, 2), lax.rem(2 * q + 3, 4))
            x_lines(line, extra_x, finish, q, 0, halo_xa)

            @pl.when((q > 0) & (t + 1 < STEPS))
            def _():
                for d in range(2):
                    copy_x(t + 1, d, 1).start()

            @pl.when(q == 0)
            def _():
                wait_x(2)

            prepare_x(t, lax.rem(2 * q + 2, 4), lax.rem(q + 1, 2), 0, halo_xa)
            pack_block_x(faces_xa, q, 2 * q)
            x_lines(line, extra_x, finish, q, 1, halo_xb)

            @pl.when(t + 1 < STEPS)
            def _():
                for d in range(2):
                    copy_x(t + 1, d, 2 * q).start()

            return carry

        lax.fori_loop(0, 2, x_body, 0)
        pack_block_x(faces_xb, 1, 3)

        @pl.when(t + 1 < STEPS)
        def _():
            for d in range(2):
                copy_x(t + 1, d, 3).start()

    def advect_step(t, carry):
        def after_z():
            @pl.when(t == 0)
            def _():
                ar_start(1, ar_finish(0))

        def after_y():
            @pl.when(t == 0)
            def _():
                top = ar_finish(1)
                top = jnp.max(jnp.max(top, axis=1, keepdims=True), axis=0, keepdims=True)
                step_s[...] = jnp.broadcast_to((CFL / 6.0) / top, (16, LANES))

        old = jnp.where(t == 0, 0.0, jnp.where(t == 1, 0.75, 1.0 / 3.0))
        new = jnp.where(t == 0, 1.0, jnp.where(t == 1, 0.25, 2.0 / 3.0))

        def finish(g, x, rows, cell, total):
            value = old * p0[g, x, rows, :] + new * (cell - step_s[...] * total)
            pc[g, x, rows, :] = value
            adv[g, x, rows, :] = value
            sgn[g, x, rows, :] = jnp.where(value > 0, 1.0, -1.0)
            return value

        run(
            t,
            advect_line,
            lambda g, i, z: pair(vz, g, i, z),
            lambda g, i, y: pair(vel.at[1], g, i, y),
            lambda g, x, rows: vel[0, g, x, rows, :],
            finish,
            after_z,
            after_y,
        )
        return carry

    lax.fori_loop(0, STAGES, advect_step, 0)

    adv_copies = [
        pltpu.make_async_copy(adv.at[g], adv_out.at[:, :, lanes(g)], out_sem.at[g]) for g in range(GROUPS)
    ]
    for copy in adv_copies:
        copy.start()

    def reinit_step(k, carry):
        def finish(g, x, rows, cell, total):
            v = adv[g, x, rows, :]
            sign = v * lax.rsqrt(v * v + 1.0)
            root = total * (1.0 / 36.0) + ROOT_EPS
            value = cell + (DTAU * sign) * (1.0 - root * lax.rsqrt(root))
            pc[g, x, rows, :] = value
            return value

        run(
            STAGES + k,
            reinit_line,
            lambda g, i, z: turned_pair(sgn, g, i, z),
            lambda g, i, y: pair(sgn, g, i, y),
            lambda g, x, rows: sgn[g, x, rows, :],
            finish,
        )
        return carry

    lax.fori_loop(0, REINIT, reinit_step, 0)

    out_copies = [
        pltpu.make_async_copy(pc.at[g], out_ref.at[:, :, lanes(g)], out_sem.at[GROUPS + g]) for g in range(GROUPS)
    ]
    for copy in out_copies:
        copy.start()
    for copy in adv_copies + out_copies:
        copy.wait()


def hand_over(a_ref, b_ref, x_ref, y_ref, buf, sem):
    ins, outs = [], []
    for k in range(4):
        part = pl.ds(2 * k, 2)
        for i, (src, dst) in enumerate(((a_ref, x_ref), (b_ref, y_ref))):
            ins.append(pltpu.make_async_copy(src.at[part], buf.at[i, part], sem.at[0, 2 * k + i]))
            outs.append(pltpu.make_async_copy(buf.at[i, part], dst.at[part], sem.at[1, 2 * k + i]))
    for copy in ins:
        copy.start()
    for arrived, onward in zip(ins, outs):
        arrived.wait()
        onward.start()
    for copy in outs:
        copy.wait()


def solution(mesh):
    n_band, n_sub = mesh.shape["band"], mesh.shape["sub"]
    low = min(4, n_band)
    cells = (GROUPS, 8, 64, LANES)

    def local(level_set, velocity, neighbours):
        whole = jax.ShapeDtypeStruct((8, 64, TILES_DEV), F32)
        anywhere = pl.BlockSpec(memory_space=pl.ANY)
        advected, reinitialized = pl.pallas_call(
            functools.partial(kernel, n_band, n_sub, low),
            out_shape=(whole, whole),
            in_specs=[anywhere, anywhere, pl.BlockSpec(memory_space=pltpu.VMEM)],
            out_specs=(anywhere, anywhere),
            scratch_shapes=[
                pltpu.VMEM(cells, F32),
                pltpu.VMEM(cells, F32),
                pltpu.VMEM(cells, F32),
                pltpu.VMEM(cells, F32),
                pltpu.VMEM((3,) + cells, F32),
                pltpu.VMEM(cells, F32),
                pltpu.VMEM(cells, F32),
                pltpu.VMEM(cells, F32),
                pltpu.VMEM((2, GROUPS, 2, 2, BLOCK, LANES), F32),
                pltpu.VMEM((2, GROUPS, 4, BLOCK, LANES), F32),
                *[pltpu.VMEM((2, GROUPS, BLOCK, LANES), F32)] * 6,
                *[pltpu.VMEM((2, 2, 2 * BLOCK, TILES_DEV), BF16)] * 2,
                pltpu.VMEM((2, 4, 128, TILES_DEV), BF16),
                pltpu.VMEM((6, TILES_DEV, TILES_DEV), BF16),
                pltpu.VMEM((2, TILES_DEV, SLOTS_X), BF16),
                pltpu.VMEM((2, TILES_DEV, LANES), BF16),
                pltpu.VMEM((2, SLOTS_X, TILES_DEV), BF16),
                pltpu.VMEM((2, LANES, TILES_DEV), BF16),
                pltpu.VMEM((TILES_DEV, TILES_DEV), BF16),
                pltpu.VMEM((6, GROUPS, 16, LANES), F32),
                pltpu.VMEM((8, TILES_DEV), jnp.int32),
                pltpu.VMEM((2, 8, TILES_DEV), jnp.int32),
                pltpu.VMEM((LANES, TILES_DEV), F32),
                pltpu.VMEM((TILES_DEV, LANES), F32),
                pltpu.VMEM((2, 4, BLOCK, SLOTS_X), F32),
                pltpu.VMEM((2, BLOCK, LANES), F32),
                pltpu.VMEM((STEPS, 2, 4, BLOCK, SLOTS_X), F32),
                pltpu.VMEM((STEPS, 2, BLOCK, LANES), F32),
                pltpu.VMEM((2, 8, LANES), F32),
                pltpu.VMEM((max(1, low * n_sub - 1), 8, LANES), F32),
                pltpu.VMEM((max(1, n_band // low - 1), 8, LANES), F32),
                pltpu.VMEM((16, LANES), F32),
                pltpu.SemaphoreType.DMA((16,)),
                pltpu.SemaphoreType.DMA((2 * GROUPS,)),
                pltpu.SemaphoreType.DMA((2, 4)),
                pltpu.SemaphoreType.DMA((STEPS, 2, 4)),
                pltpu.SemaphoreType.DMA((2,)),
                pltpu.SemaphoreType.DMA((STEPS, 2)),
                pltpu.SemaphoreType.DMA((low * n_sub + n_band // low,)),
                pltpu.SemaphoreType.DMA((low * n_sub + n_band // low,)),
            ],
            compiler_params=pltpu.CompilerParams(
                collective_id=0, has_side_effects=True, vmem_limit_bytes=56 * 2**20
            ),
        )(level_set.reshape(8, 64, TILES_DEV), velocity.reshape(3, 8, 64, TILES_DEV), neighbours)
        advected, reinitialized = pl.pallas_call(
            hand_over,
            out_shape=(whole, whole),
            in_specs=[anywhere, anywhere],
            out_specs=(anywhere, anywhere),
            scratch_shapes=[pltpu.VMEM((2, 8, 64, TILES_DEV), F32), pltpu.SemaphoreType.DMA((2, 8))],
        )(advected, reinitialized)
        return advected.reshape(8, 8, 8, TILES_DEV), reinitialized.reshape(8, 8, 8, TILES_DEV)

    return jax.shard_map(
        local,
        mesh=mesh,
        in_specs=(
            P(None, None, None, ("band", "sub")),
            P(None, None, None, None, ("band", "sub")),
            P(None, ("band", "sub")),
        ),
        out_specs=(P(None, None, None, ("band", "sub")), P(None, None, None, ("band", "sub"))),
        check_vma=False,
    )
```

time: 80.3 us -> 71.8 us (0.89)
  Pallas kernels: 79.4 us -> 71 us
    pallas_call x1, Pallas kernels: 77 us -> 68.6 us  [local(): pl.pallas_call(functools.partial(kernel, n_band, n_sub, low), out_shape=(...]
where the time goes in v2:
time: 71.8 us; the launch traced here: 71.6 us
  Pallas kernels  71 us (99%)
    pallas_call x1, Pallas kernels, local(): pl.pallas_call(functools.partial(kernel, n_band, n_sub, low), out_shape=(...  68.6 us
    pallas_call x1, Pallas kernels, local(): pl.pallas_call(hand_over, out_shape=(whole, whole), in_specs=[anywhere, a...  2.4 us

profile of v2, /device:TPU:0, one launch (start us, length us, event | category | flops | bytes accessed | tf_op | source)
XLA Modules:
  0.0 71.6 jit_solution(349599832039180917)
XLA Ops:
  0.6 68.6 %shard_map.50 = (f32[8,64,512]{2,1,0:T(8,128)}, f32[8,64,512]{2,1,0:T(8,128)}) custom-call(f32[8,64,512]{2,1,0:T(8,128)} %bitcast.5, f32[3,8,64,512]{3,2,1,0:T(8,128)} %bitcast.4, s32[6,512]{1,0:T(8,128)} %nb_ref.1), custom_call_target="tpu_custom_call" | custom-call | tf_op jit(solution)/shard_map/pallas_call | solution.py:610
  69.2 2.4 %shard_map.51 = (f32[8,64,512]{2,1,0:T(8,128)}, f32[8,64,512]{2,1,0:T(8,128)}) custom-call(f32[8,64,512]{2,1,0:T(8,128)} %get-tuple-element.6.a_ref, f32[8,64,512]{2,1,0:T(8,128)} %get-tuple-element.7.b_ref), custom_call_target="tpu_custom_call" | custom-call | tf_op jit(solution)/shard_map/pallas_call | solution.py:661

commit v3 on v2

--- a/solution.py
+++ b/solution.py
@@ -115,7 +115,7 @@
     n_band, n_sub, low,
     ls_ref, vel_ref, nb_ref, adv_out, out_ref,
     p0, pc, adv, sgn, vel, vz, az, ay,
-    local_x, local_y, halo_xa, halo_xb, halo_ya, halo_yb, halo_za, halo_zb, faces_xa, faces_xb, faces_y,
+    halo_xa, halo_xb, halo_ya, halo_yb, halo_za, halo_zb, faces_x, faces_y, faces_z, came_x, came_y,
     local_m, pack_x, pack_y, unpack_x, unpack_y, tri, pres,
     nb_s, ids_s, krow, kcol, send_x, send_y, recv_x, recv_y, ar_send, ar_near, ar_far, step_s,
     in_sem, out_sem, tx_x, rx_x, tx_y, rx_y, ar_tx, ar_rx,
@@ -266,10 +266,26 @@
     lax.fori_loop(0, TILES_DEV // 64, fill_pack, 0)
 
     def put_face(ref, lead, l, col, hi, lo):
-        ref[(*lead, pl.ds(16 * l, 16), col)] = hi
-        ref[(*lead, pl.ds(BLOCK + 16 * l, 16), col)] = lo
-
-    def put_faces_xy(g, q, odd, values):
+        ref[(*lead, pl.ds(pl.multiple_of(16 * l, 16), 16), col)] = hi
+        ref[(*lead, pl.ds(pl.multiple_of(BLOCK + 16 * l, 16), 16), col)] = lo
+
+    def outer_block(k):
+        return [(pl.multiple_of(48 * k, 16), 16)], ((1 - k, k), (1 - k, k + 1))
+
+    third_block = [(16, 8), (40, 8)], ((1, 2), (0, 0))
+    fourth_block = [(24, 16)], ()
+
+    def take(ref, lead, rows):
+        pieces = [ref[(*lead, pl.ds(start, size), slice(None))] for start, size in rows]
+        return pieces[0] if len(pieces) == 1 else jnp.concatenate(pieces, axis=0)
+
+    def put(ref, lead, rows, value):
+        first = 0
+        for start, size in rows:
+            ref[(*lead, pl.ds(start, size), slice(None))] = value[first : first + size]
+            first += size
+
+    def put_faces_xy(g, c, y_faces, values):
         col = pl.ds(g * LANES, LANES)
         parts = []
         for x in range(8):
@@ -277,37 +293,47 @@
             rest = values[x] - hi.astype(F32)
             parts.append(rest)
             if x not in (3, 4):
-                put_face(faces_xb if odd else faces_xa, (0 if x > 4 else 1, q), x - 5 if x > 4 else x, col, hi, rest.astype(BF16))
-        for j in range(2):
+                put_face(faces_x, (0 if x > 4 else 1, c), x - 5 if x > 4 else x, col, hi, rest.astype(BF16))
+        for j, (d, layer) in enumerate(y_faces):
             for i in range(4):
                 hi, lo = [
                     jnp.concatenate([part[2 * i + e][8 * j : 8 * j + 8] for e in range(2)], axis=0).astype(BF16)
                     for part in (values, parts)
                 ]
-                row = 2 * odd + j
-                faces_y[q, i, pl.ds(16 * row, 16), col] = hi
-                faces_y[q, i, pl.ds(64 + 16 * row, 16), col] = lo
-
-    def pack_block_x(ref, q, r):
+                put_face(faces_y, (d, i), layer, col, hi, lo)
+
+    def pack_block_x(c):
         for d in range(2):
-            send_x[d, r] = two_part_dot(ref[1 - d, q], pack_x[d])[0]
-
-    def copy_in(q, carry):
-        for odd in range(2):
-            for g in range(GROUPS):
-                rows = pl.ds(pl.multiple_of(32 * q + 16 * odd, 16), 16)
-                values = [p0[g, x, rows, :] for x in range(8)]
-                for x in range(8):
-                    pc[g, x, rows, :] = values[x]
-                put_faces_xy(g, q, odd, values)
-            pack_block_x(faces_xb if odd else faces_xa, q, 2 * q + odd)
-            for d in range(2):
-                copy_x(0, d, 2 * q + odd).start()
+            send_x[d, c] = two_part_dot(faces_x[1 - d, c], pack_x[d])[0]
+
+    def pack_y_faces():
+        for d in range(2):
+            parts = two_part_dot(faces_y[1 - d].reshape(8 * BLOCK, TILES_DEV), pack_y[d])
+            send_y[d] = sum(pltpu.roll(parts[i], i * SLOTS_Y, 1) if i else parts[i] for i in range(4))
+
+    def copy_in(c, block):
+        rows, y_faces = block
+        for g in range(GROUPS):
+            values = [take(p0, (g, x), rows) for x in range(8)]
+            for x in range(8):
+                put(pc, (g, x), rows, values[x])
+            put_faces_xy(g, c, y_faces, values)
+        pack_block_x(c)
+        for d in range(2):
+            copy_x(0, d, c).start()
+
+    def copy_in_outer(k, carry):
+        copy_in(k, outer_block(k))
         return carry
 
     for copy in in_copies[3 * GROUPS :]:
         copy.wait()
-    lax.fori_loop(0, 2, copy_in, 0)
+    lax.fori_loop(0, 2, copy_in_outer, 0)
+    copy_in(2, third_block)
+    pack_y_faces()
+    for d in range(2):
+        copy_y(0, d).start()
+    copy_in(3, fourth_block)
 
     def fill(k, carry):
         for j in range(2):
@@ -352,163 +378,173 @@
         return jnp.concatenate([ref[g, 2 * i + j, pl.ds(k, 8, stride=8), :] for j in range(2)], axis=0)
 
     def pair(ref, g, i, k):
-        return ref[g, pl.ds(2 * i, 2), 8 * k : 8 * k + 8, :].reshape(16, LANES)
-
-    def face_y(d, i):
-        first = 16 * (1 - d)
-        return jnp.concatenate(
-            [faces_y[1 - d, i, pl.ds(pl.multiple_of(64 * part + first, 16), BLOCK), :] for part in range(2)], axis=0
-        )
-
-    def put_halo(halo, d, res, local):
+        return ref[g, 2 * i : 2 * i + 2, 8 * k : 8 * k + 8, :].reshape(16, LANES)
+
+    def put_faces_z():
         for g in range(GROUPS):
-            part = res[:, g * LANES : (g + 1) * LANES]
-            halo[d, g] = part if local is None else part + local[g]
-
-    def prepare_z(i, halo):
-        for d, start in ((0, 5), (1, 0)):
-            value = jnp.concatenate(
-                [
-                    jnp.concatenate([turned_pair(pc, g, i, start + l) for g in range(GROUPS)], axis=1)
-                    for l in range(3)
-                ],
-                axis=0,
-            )
-            put_halo(halo, d, two_part_dot(split_rows(value), local_m[4 + d])[0], None)
-
-    def prepare_y(t, i, halo):
+            col = pl.ds(g * LANES, LANES)
+            for i in range(4):
+                for d, start in ((0, 5), (1, 0)):
+                    for l in range(3):
+                        value = turned_pair(pc, g, i, start + l)
+                        hi = value.astype(BF16)
+                        put_face(faces_z, (d, i), l, col, hi, (value - hi.astype(F32)).astype(BF16))
+
+    def group_of(res, g):
+        return res[:, g * LANES : (g + 1) * LANES]
+
+    def gather_z(d, half, halo):
+        faces = faces_z[d].reshape(8 * BLOCK, TILES_DEV)
+        for i, res in enumerate(two_part_dot(faces, local_m[4 + d, :, 2 * half * LANES : 2 * (half + 1) * LANES])):
+            for g in range(2):
+                halo[d, g, i] = group_of(res, g)
+
+    def gather_y(d):
+        for i, res in enumerate(two_part_dot(faces_y[d].reshape(8 * BLOCK, TILES_DEV), local_m[2 + d])):
+            for g in range(GROUPS):
+                (halo_ya, halo_yb)[g // 2][d, g % 2, i] = group_of(res, g)
+
+    def gather_x(d):
+        for r, res in enumerate(two_part_dot(faces_x[d].reshape(8 * BLOCK, TILES_DEV), local_m[d])):
+            for g in range(GROUPS):
+                (halo_xa, halo_xb)[r // 2][d, r % 2, g] = group_of(res, g)
+
+    def split_y(t):
         for d in range(2):
-            block = pltpu.roll(recv_y[t, d], lax.rem((4 - i) * SLOTS_Y, LANES), 1)
-            res = two_part_dot(split_rows(block), unpack_y[d])[0]
-            put_halo(halo, d, res, [local_y[d, g, i] for g in range(GROUPS)])
-
-    def prepare_x(t, r, q, odd, halo):
+            parts = split_rows(recv_y[t, d])
+            wide = parts.astype(F32)
+            for i in range(4):
+                block = pltpu.roll(wide, LANES - i * SLOTS_Y, 1).astype(BF16) if i else parts
+                came_y[d, 2 * BLOCK * i : 2 * BLOCK * (i + 1), :] = block
+
+    def split_x(t, half):
         for d in range(2):
-            res = two_part_dot(split_rows(recv_x[t, d, r]), unpack_x[d])[0]
-            put_halo(halo, d, res, [local_x[d, g, odd, q] for g in range(GROUPS)])
-
-    def gather_y(d):
-        faces = jnp.concatenate([face_y(d, i) for i in range(4)], axis=0)
-        for i, res in enumerate(two_part_dot(faces, local_m[2 + d])):
+            for k in range(2):
+                came_x[d, half, 2 * BLOCK * k : 2 * BLOCK * (k + 1), :] = split_rows(recv_x[t, d, 2 * half + k])
+
+    def unpack_half_y(d, half, halo):
+        matrix = unpack_y[d, :, 2 * half * LANES : 2 * (half + 1) * LANES]
+        for i, res in enumerate(two_part_dot(came_y[d], matrix)):
+            for g in range(2):
+                halo[d, g, i] = halo[d, g, i] + group_of(res, g)
+
+    def unpack_half_x(d, half, halo):
+        for k, res in enumerate(two_part_dot(came_x[d, half], unpack_x[d])):
             for g in range(GROUPS):
-                local_y[d, g, i] = res[:, g * LANES : (g + 1) * LANES]
-
-    def gather_x(d):
-        faces = jnp.concatenate([ref[d, q] for ref in (faces_xa, faces_xb) for q in range(2)], axis=0)
-        for k, res in enumerate(two_part_dot(faces, local_m[d])):
-            for g in range(GROUPS):
-                local_x[d, g, k // 2, k % 2] = res[:, g * LANES : (g + 1) * LANES]
-
-    def padded(halo, there, g, cells):
+                halo[d, k, g] = halo[d, k, g] + group_of(res, g)
+
+    def padded(halo, a, b, there, g, cells):
         there_lo = pres[there, g] > 0
         there_hi = pres[there + 1, g] > 0
-        before = [jnp.where(there_lo, halo[0, g, 16 * l : 16 * l + 16, :], cells[0]) for l in range(3)]
-        after = [jnp.where(there_hi, halo[1, g, 16 * l : 16 * l + 16, :], cells[7]) for l in range(3)]
+        before = [jnp.where(there_lo, halo[0, a, b, 16 * l : 16 * l + 16, :], cells[0]) for l in range(3)]
+        after = [jnp.where(there_hi, halo[1, a, b, 16 * l : 16 * l + 16, :], cells[7]) for l in range(3)]
         return before + cells + after
 
-    def z_lines(line, extra, i, halo):
-        for g in range(GROUPS):
+    def z_lines(line, extra, half, k, halo):
+        g = 2 * half + k
+        for i in range(4):
             cells = [turned_pair(pc, g, i, z) for z in range(8)]
-            values = line(padded(halo, 4, g, cells), [extra(g, i, z) for z in range(8)])
+            values = line(padded(halo, k, i, 4, g, cells), [extra(g, i, z) for z in range(8)])
             for z in range(8):
-                az[g, pl.ds(2 * i, 2), 8 * z : 8 * z + 8, :] = values[z].reshape(2, 8, LANES)
-
-    def y_lines(line, extra, i, halo):
-        for g in range(GROUPS):
+                az[g, 2 * i : 2 * i + 2, 8 * z : 8 * z + 8, :] = values[z].reshape(2, 8, LANES)
+
+    def y_lines(line, extra, half, k, halo):
+        g = 2 * half + k
+        for i in range(4):
             cells = [pair(pc, g, i, y) for y in range(8)]
-            values = line(padded(halo, 2, g, cells), [extra(g, i, y) for y in range(8)])
+            values = line(padded(halo, k, i, 2, g, cells), [extra(g, i, y) for y in range(8)])
             for y in range(8):
                 total = values[y] + turned_pair(az, g, i, y)
-                ay[g, pl.ds(2 * i, 2), 8 * y : 8 * y + 8, :] = total.reshape(2, 8, LANES)
-
-    def x_lines(line, extra, finish, q, odd, halo):
-        rows = pl.ds(pl.multiple_of(32 * q + 16 * odd, 16), 16)
-        ahead = [pc[0, x, rows, :] for x in range(8)]
-        for g in range(GROUPS):
+                ay[g, 2 * i : 2 * i + 2, 8 * y : 8 * y + 8, :] = total.reshape(2, 8, LANES)
+
+    def x_lines(line, extra, finish, c, block, halo, k, groups=range(GROUPS)):
+        rows, y_faces = block
+        ahead = [take(pc, (groups[0], x), rows) for x in range(8)]
+        for g in groups:
             cells = ahead
-            if g + 1 < GROUPS:
-                ahead = [pc[g + 1, x, rows, :] for x in range(8)]
-            values = line(padded(halo, 0, g, cells), [extra(g, x, rows) for x in range(8)])
-            fresh = [finish(g, x, rows, cells[x], values[x] + ay[g, x, rows, :]) for x in range(8)]
-            put_faces_xy(g, q, odd, fresh)
+            if g + 1 in groups:
+                ahead = [take(pc, (g + 1, x), rows) for x in range(8)]
+            values = line(padded(halo, k, g, 0, g, cells), [extra(g, x, rows) for x in range(8)])
+            fresh = [finish(g, x, rows, cells[x], values[x] + take(ay, (g, x), rows)) for x in range(8)]
+            put_faces_xy(g, c, y_faces, fresh)
+
+    def twice(body):
+        def step(k, carry):
+            body(k)
+            return carry
+
+        lax.fori_loop(0, 2, step, 0)
 
     def run(t, line, extra_z, extra_y, extra_x, finish, after_z=None, after_y=None):
-        for d in range(2):
-            parts = [two_part_dot(face_y(1 - d, i), pack_y[d])[0] for i in range(4)]
-            send_y[d] = sum(pltpu.roll(parts[i], i * SLOTS_Y, 1) if i else parts[i] for i in range(4))
-            copy_y(t, d).start()
-        prepare_z(0, halo_za)
-
-        def z_body(q, carry):
-            prepare_z(2 * q + 1, halo_zb)
-            gather_y(q)
-            z_lines(line, extra_z, 2 * q, halo_za)
-            prepare_z(lax.rem(2 * q + 2, 4), halo_za)
-            z_lines(line, extra_z, 2 * q + 1, halo_zb)
-            return carry
-
-        lax.fori_loop(0, 2, z_body, 0)
+        put_faces_z()
+        gather_z(0, 0, halo_za)
+        gather_z(1, 0, halo_za)
+
+        def z_first(k):
+            gather_z(k, 1, halo_zb)
+            z_lines(line, extra_z, 0, k, halo_za)
+
+        def z_second(k):
+            gather_y(k)
+            z_lines(line, extra_z, 1, k, halo_zb)
+
+        twice(z_first)
+        twice(z_second)
         if after_z is not None:
             after_z()
         for d in range(2):
             copy_y(t, d).wait()
-        prepare_y(t, 0, halo_ya)
-
-        def y_body(q, carry):
-            prepare_y(t, 2 * q + 1, halo_yb)
-            gather_x(q)
-            y_lines(line, extra_y, 2 * q, halo_ya)
-            prepare_y(t, lax.rem(2 * q + 2, 4), halo_ya)
-            y_lines(line, extra_y, 2 * q + 1, halo_yb)
-            return carry
-
-        lax.fori_loop(0, 2, y_body, 0)
+        split_y(t)
+        unpack_half_y(0, 0, halo_ya)
+        unpack_half_y(1, 0, halo_ya)
+
+        def y_first(k):
+            gather_x(k)
+            unpack_half_y(k, 1, halo_yb)
+            y_lines(line, extra_y, 0, k, halo_ya)
+
+        def y_second(k):
+            unpack_half_x(k, 0, halo_xa)
+            y_lines(line, extra_y, 1, k, halo_yb)
+
+        twice(y_first)
+        for r in range(2):
+            for d in range(2):
+                copy_x(t, d, r).wait()
+        split_x(t, 0)
+        twice(y_second)
         if after_y is not None:
             after_y()
-
-        def wait_x(r):
+        for r in range(2, 4):
             for d in range(2):
-                copy_x(t, d, r).wait_recv()
-
-        for r in range(4):
-            for d in range(2):
-                copy_x(t, d, r).wait_send()
-        wait_x(0)
-        prepare_x(t, 0, 0, 0, halo_xa)
-
-        def x_body(q, carry):
-            wait_x(2 * q + 1)
-            prepare_x(t, 2 * q + 1, q, 1, halo_xb)
-            pack_block_x(faces_xb, lax.rem(q + 1, 2), lax.rem(2 * q + 3, 4))
-            x_lines(line, extra_x, finish, q, 0, halo_xa)
-
-            @pl.when((q > 0) & (t + 1 < STEPS))
-            def _():
-                for d in range(2):
-                    copy_x(t + 1, d, 1).start()
-
-            @pl.when(q == 0)
-            def _():
-                wait_x(2)
-
-            prepare_x(t, lax.rem(2 * q + 2, 4), lax.rem(q + 1, 2), 0, halo_xa)
-            pack_block_x(faces_xa, q, 2 * q)
-            x_lines(line, extra_x, finish, q, 1, halo_xb)
-
+                copy_x(t, d, r).wait()
+
+        split_x(t, 1)
+
+        def send_on(copies):
             @pl.when(t + 1 < STEPS)
             def _():
-                for d in range(2):
-                    copy_x(t + 1, d, 2 * q).start()
-
-            return carry
-
-        lax.fori_loop(0, 2, x_body, 0)
-        pack_block_x(faces_xb, 1, 3)
-
-        @pl.when(t + 1 < STEPS)
-        def _():
-            for d in range(2):
-                copy_x(t + 1, d, 3).start()
+                for copy in copies():
+                    copy.start()
+
+        def x_outer(k):
+            unpack_half_x(k, 1, halo_xb)
+            pack_block_x(lax.rem(k + 3, 4))
+            x_lines(line, extra_x, finish, k, outer_block(k), halo_xa, k)
+
+        twice(x_outer)
+        send_on(lambda: [copy_x(t + 1, d, 0) for d in range(2)])
+        pack_block_x(1)
+        x_lines(line, extra_x, finish, 2, third_block, halo_xb, 0)
+        send_on(lambda: [copy_x(t + 1, d, 1) for d in range(2)])
+        pack_y_faces()
+        x_lines(line, extra_x, finish, 3, fourth_block, halo_xb, 1, range(2))
+        send_on(lambda: [copy_y(t + 1, d) for d in range(2)])
+        pack_block_x(2)
+        x_lines(line, extra_x, finish, 3, fourth_block, halo_xb, 1, range(2, 4))
+        send_on(lambda: [copy_x(t + 1, d, 2) for d in range(2)])
+        pack_block_x(3)
+        send_on(lambda: [copy_x(t + 1, d, 3) for d in range(2)])
 
     def advect_step(t, carry):
         def after_z():
@@ -527,10 +563,10 @@
         new = jnp.where(t == 0, 1.0, jnp.where(t == 1, 0.25, 2.0 / 3.0))
 
         def finish(g, x, rows, cell, total):
-            value = old * p0[g, x, rows, :] + new * (cell - step_s[...] * total)
-            pc[g, x, rows, :] = value
-            adv[g, x, rows, :] = value
-            sgn[g, x, rows, :] = jnp.where(value > 0, 1.0, -1.0)
+            value = old * take(p0, (g, x), rows) + new * (cell - step_s[...] * total)
+            put(pc, (g, x), rows, value)
+            put(adv, (g, x), rows, value)
+            put(sgn, (g, x), rows, jnp.where(value > 0, 1.0, -1.0))
             return value
 
         run(
@@ -538,7 +574,7 @@
             advect_line,
             lambda g, i, z: pair(vz, g, i, z),
             lambda g, i, y: pair(vel.at[1], g, i, y),
-            lambda g, x, rows: vel[0, g, x, rows, :],
+            lambda g, x, rows: take(vel, (0, g, x), rows),
             finish,
             after_z,
             after_y,
@@ -555,11 +591,11 @@
 
     def reinit_step(k, carry):
         def finish(g, x, rows, cell, total):
-            v = adv[g, x, rows, :]
+            v = take(adv, (g, x), rows)
             sign = v * lax.rsqrt(v * v + 1.0)
             root = total * (1.0 / 36.0) + ROOT_EPS
             value = cell + (DTAU * sign) * (1.0 - root * lax.rsqrt(root))
-            pc[g, x, rows, :] = value
+            put(pc, (g, x), rows, value)
             return value
 
         run(
@@ -567,7 +603,7 @@
             reinit_line,
             lambda g, i, z: turned_pair(sgn, g, i, z),
             lambda g, i, y: pair(sgn, g, i, y),
-            lambda g, x, rows: sgn[g, x, rows, :],
+            lambda g, x, rows: take(sgn, (g, x), rows),
             finish,
         )
         return carry
@@ -621,11 +657,13 @@
                 pltpu.VMEM(cells, F32),
                 pltpu.VMEM(cells, F32),
                 pltpu.VMEM(cells, F32),
-                pltpu.VMEM((2, GROUPS, 2, 2, BLOCK, LANES), F32),
-                pltpu.VMEM((2, GROUPS, 4, BLOCK, LANES), F32),
-                *[pltpu.VMEM((2, GROUPS, BLOCK, LANES), F32)] * 6,
-                *[pltpu.VMEM((2, 2, 2 * BLOCK, TILES_DEV), BF16)] * 2,
-                pltpu.VMEM((2, 4, 128, TILES_DEV), BF16),
+                *[pltpu.VMEM((2, 2, GROUPS, BLOCK, LANES), F32)] * 2,
+                *[pltpu.VMEM((2, 2, 4, BLOCK, LANES), F32)] * 4,
+                pltpu.VMEM((2, 4, 2 * BLOCK, TILES_DEV), BF16),
+                pltpu.VMEM((2, 4, 2 * BLOCK, TILES_DEV), BF16),
+                pltpu.VMEM((2, 4, 2 * BLOCK, TILES_DEV), BF16),
+                pltpu.VMEM((2, 2, 4 * BLOCK, SLOTS_X), BF16),
+                pltpu.VMEM((2, 8 * BLOCK, LANES), BF16),
                 pltpu.VMEM((6, TILES_DEV, TILES_DEV), BF16),
                 pltpu.VMEM((2, TILES_DEV, SLOTS_X), BF16),
                 pltpu.VMEM((2, TILES_DEV, LANES), BF16),

time: 71.8 us -> 65.3 us (0.909)
  Pallas kernels: 71 us -> 64.4 us
    pallas_call x1, Pallas kernels: 68.6 us -> 62 us  [local(): pl.pallas_call(functools.partial(kernel, n_band, n_sub, low), out_shape=(...]
where the time goes in v3:
time: 65.3 us; the launch traced here: 65.1 us
  Pallas kernels  64.4 us (99%)
    pallas_call x1, Pallas kernels, local(): pl.pallas_call(functools.partial(kernel, n_band, n_sub, low), out_shape=(...  62 us
    pallas_call x1, Pallas kernels, local(): pl.pallas_call(hand_over, out_shape=(whole, whole), in_specs=[anywhere, a...  2.4 us

profile of v3, /device:TPU:0, one launch (start us, length us, event | category | flops | bytes accessed | tf_op | source)
XLA Modules:
  0.0 65.1 jit_solution(4861254722450649453)
XLA Ops:
  0.6 62.0 %shard_map.50 = (f32[8,64,512]{2,1,0:T(8,128)}, f32[8,64,512]{2,1,0:T(8,128)}) custom-call(f32[8,64,512]{2,1,0:T(8,128)} %bitcast.5, f32[3,8,64,512]{3,2,1,0:T(8,128)} %bitcast.4, s32[6,512]{1,0:T(8,128)} %nb_ref.1), custom_call_target="tpu_custom_call" | custom-call | tf_op jit(solution)/shard_map/pallas_call | solution.py:646
  62.7 2.4 %shard_map.51 = (f32[8,64,512]{2,1,0:T(8,128)}, f32[8,64,512]{2,1,0:T(8,128)}) custom-call(f32[8,64,512]{2,1,0:T(8,128)} %get-tuple-element.6.a_ref, f32[8,64,512]{2,1,0:T(8,128)} %get-tuple-element.7.b_ref), custom_call_target="tpu_custom_call" | custom-call | tf_op jit(solution)/shard_map/pallas_call | solution.py:699

commit v4 on v3

--- a/solution.py
+++ b/solution.py
@@ -26,74 +26,106 @@
 MESH = pl.DeviceIdType.MESH
 
 
-def differences(p):
-    first = [p[k + 1] - p[k] for k in range(13)]
-    second = [first[k + 1] - first[k] for k in range(12)]
-    third = [second[k + 1] - second[k] for k in range(11)]
-    fourth = [None] + [third[k] - third[k - 1] for k in range(1, 11)]
-    square = [e * e for e in second]
-    ind_a, ind_b, ind_c = {}, {}, {}
-    for k in range(11):
-        half = (0.5 * second[k]) * second[k + 1]
-        base = third[k] * third[k] * (2.0 / 3.0) + 0.5 * EPS
-        low = base - half
-        if k <= 8:
-            ind_a[k] = low + square[k + 1]
-        if 1 <= k <= 9:
-            ind_b[k] = base + half
-        if k >= 2:
-            ind_c[k] = low + square[k]
-    return third, fourth, ind_a, ind_b, ind_c
+class Line:
+    def __init__(self, cell):
+        self.cell, self.made = cell, {}
+
+    def get(self, kind, k):
+        if (kind, k) not in self.made:
+            self.made[kind, k] = getattr(self, kind)(k)
+        return self.made[kind, k]
+
+    def first(self, k):
+        return self.get("cell", k + 1) - self.get("cell", k)
+
+    def second(self, k):
+        return self.get("first", k + 1) - self.get("first", k)
+
+    def third(self, k):
+        return self.get("second", k + 1) - self.get("second", k)
+
+    def fourth(self, k):
+        return self.get("third", k) - self.get("third", k - 1)
+
+    def square(self, k):
+        return self.get("second", k) * self.get("second", k)
+
+    def half(self, k):
+        return (0.5 * self.get("second", k)) * self.get("second", k + 1)
+
+    def base(self, k):
+        return self.get("third", k) * self.get("third", k) * (2.0 / 3.0) + 0.5 * EPS
+
+    def low(self, k):
+        return self.get("base", k) - self.get("half", k)
+
+    def ind_a(self, k):
+        return self.get("low", k) + self.get("square", k + 1)
+
+    def ind_b(self, k):
+        return self.get("base", k) + self.get("half", k)
+
+    def ind_c(self, k):
+        return self.get("low", k) + self.get("square", k)
+
+    def weight_a(self, k):
+        r = recip(self.get("ind_a", k))
+        return r * r
+
+    def weight_b(self, k):
+        r = recip(self.get("ind_b", k))
+        return r * r * 6.0
+
+    def weight_c(self, k):
+        r = recip(self.get("ind_c", k))
+        return r * r
+
+    def triple_a(self, k):
+        return self.get("weight_a", k) * 3.0
+
+    def triple_c(self, k):
+        return self.get("weight_c", k) * 3.0
+
+    def twice(self, k):
+        return self.get("fourth", k) + self.get("fourth", k)
 
 
 def recip(x):
     return pl.reciprocal(x, approx=True)
 
 
-def advect_line(p, flow):
-    third, fourth, ind_a, ind_b, ind_c = differences(p)
-    out = []
+def advect_line(cell, flow_of):
+    get = Line(cell).get
     for c in range(8):
-        up = flow[c] > 0
-        ra = recip(jnp.where(up, ind_a[c], ind_c[c + 3]))
-        rb = recip(jnp.where(up, ind_b[c + 1], ind_b[c + 2]))
-        rc = recip(jnp.where(up, ind_c[c + 2], ind_a[c + 1]))
+        flow = flow_of(c)
+        up = flow > 0
+        ra = recip(jnp.where(up, get("ind_a", c), get("ind_c", c + 3)))
+        rb = recip(jnp.where(up, get("ind_b", c + 1), get("ind_b", c + 2)))
+        rc = recip(jnp.where(up, get("ind_c", c + 2), get("ind_a", c + 1)))
         wa = ra * ra
         wb = rb * rb * 6.0
         wc = rc * rc * 3.0
-        far = jnp.where(up, fourth[c + 1], fourth[c + 3])
-        num = wa * (far + far) + wc * fourth[c + 2]
+        far = jnp.where(up, get("fourth", c + 1), get("fourth", c + 3))
+        num = wa * (far + far) + wc * get("fourth", c + 2)
         corr = num * recip(wa + wb + wc)
-        linear = 3.0 * (p[c + 4] - p[c + 2]) - jnp.where(up, third[c + 1], third[c + 2])
-        out.append(flow[c] * linear - jnp.abs(flow[c]) * corr)
-    return out
-
-
-def reinit_line(p, sign):
-    third, fourth, ind_a, ind_b, ind_c = differences(p)
-    wa, wa3, wb, wc, wc3 = {}, {}, {}, {}, {}
-    for k, v in ind_a.items():
-        r = recip(v)
-        wa[k] = r * r
-        wa3[k] = wa[k] * 3.0
-    for k, v in ind_b.items():
-        r = recip(v)
-        wb[k] = r * r * 6.0
-    for k, v in ind_c.items():
-        r = recip(v)
-        wc[k] = r * r
-        wc3[k] = wc[k] * 3.0
-    twice = [None] + [f + f for f in fourth[1:]]
-    out = []
+        linear = 3.0 * (get("cell", c + 4) - get("cell", c + 2)) - jnp.where(up, get("third", c + 1), get("third", c + 2))
+        yield flow * linear - jnp.abs(flow) * corr
+
+
+def reinit_line(cell, sign_of):
+    get = Line(cell).get
     for c in range(8):
-        linear = 3.0 * (p[c + 4] - p[c + 2])
-        corr_b = (wa[c] * twice[c + 1] + wc3[c + 2] * fourth[c + 2]) * recip(wa[c] + wb[c + 1] + wc3[c + 2])
-        corr_f = (wc[c + 3] * twice[c + 3] + wa3[c + 1] * fourth[c + 2]) * recip(wc[c + 3] + wb[c + 2] + wa3[c + 1])
-        back = linear - third[c + 1] - corr_b
-        fore = third[c + 2] - linear - corr_f
-        m = jnp.maximum(jnp.maximum(sign[c] * back, sign[c] * fore), 0.0)
-        out.append(m * m)
-    return out
+        sign = sign_of(c)
+        linear = 3.0 * (get("cell", c + 4) - get("cell", c + 2))
+        mid = get("fourth", c + 2)
+        wa, wb, wc = get("weight_a", c), get("weight_b", c + 1), get("triple_c", c + 2)
+        corr_b = (wa * get("twice", c + 1) + wc * mid) * recip(wa + wb + wc)
+        wa, wb, wc = get("weight_c", c + 3), get("weight_b", c + 2), get("triple_a", c + 1)
+        corr_f = (wa * get("twice", c + 3) + wc * mid) * recip(wa + wb + wc)
+        back = linear - get("third", c + 1) - corr_b
+        fore = get("third", c + 2) - linear - corr_f
+        m = jnp.maximum(jnp.maximum(sign * back, sign * fore), 0.0)
+        yield m * m
 
 
 def split_rows(value):
@@ -138,13 +170,13 @@
         return pl.ds(g * LANES, LANES)
 
     in_copies = []
+    for g in range(GROUPS):
+        in_copies.append(pltpu.make_async_copy(ls_ref.at[:, :, lanes(g)], p0.at[g], in_sem.at[12 + g]))
     for k in range(3):
         for g in range(GROUPS):
             in_copies.append(
                 pltpu.make_async_copy(vel_ref.at[k, :, :, lanes(g)], vel.at[k, g], in_sem.at[4 * k + g])
             )
-    for g in range(GROUPS):
-        in_copies.append(pltpu.make_async_copy(ls_ref.at[:, :, lanes(g)], p0.at[g], in_sem.at[12 + g]))
     for copy in in_copies:
         copy.start()
 
@@ -185,23 +217,6 @@
     krow[4:8, :] = jnp.where(remote, place, -1.0)[0:4]
     for c in range(GROUPS):
         kcol[c * LANES : (c + 1) * LANES, :] = krow[:, c * LANES : (c + 1) * LANES].T
-
-    for copy in in_copies[: 3 * GROUPS]:
-        copy.wait()
-
-    def speeds(idx, top):
-        g, x = idx // 8, lax.rem(idx, 8)
-        for y in range(8):
-            rows = slice(8 * y, 8 * y + 8)
-            total = jnp.abs(vel[0, g, x, rows, :]) + jnp.abs(vel[1, g, x, rows, :]) + jnp.abs(vel[2, g, x, rows, :])
-            top = jnp.maximum(top, total)
-        for z in range(8):
-            vz[g, x, 8 * z : 8 * z + 8, :] = vel[2, g, x, pl.ds(z, 8, stride=8), :]
-        return top
-
-    top = lax.fori_loop(0, GROUPS * 8, speeds, jnp.zeros((8, LANES), F32))
-
-    pl.semaphore_wait(barrier, len(peers))
 
     def ar_copies(r):
         peer, slots, n = ((near_peer, ar_near, n_near), (far_peer, ar_far, n_high))[r]
@@ -231,8 +246,6 @@
             value = jnp.maximum(value, slots[k])
         return value
 
-    ar_start(0, top)
-
     def copy_x(t, d, r):
         return pltpu.make_async_remote_copy(
             src_ref=send_x.at[d, r],
@@ -285,22 +298,26 @@
             ref[(*lead, pl.ds(start, size), slice(None))] = value[first : first + size]
             first += size
 
-    def put_faces_xy(g, c, y_faces, values):
+    def put_faces_xy(g, c, y_faces):
         col = pl.ds(g * LANES, LANES)
-        parts = []
-        for x in range(8):
-            hi = values[x].astype(BF16)
-            rest = values[x] - hi.astype(F32)
-            parts.append(rest)
+        kept = []
+
+        def add(x, value):
+            hi = value.astype(BF16)
+            rest = value - hi.astype(F32)
+            kept.append((value, rest))
             if x not in (3, 4):
                 put_face(faces_x, (0 if x > 4 else 1, c), x - 5 if x > 4 else x, col, hi, rest.astype(BF16))
-        for j, (d, layer) in enumerate(y_faces):
-            for i in range(4):
+            if x % 2 == 0:
+                return
+            for j, (d, layer) in enumerate(y_faces):
                 hi, lo = [
-                    jnp.concatenate([part[2 * i + e][8 * j : 8 * j + 8] for e in range(2)], axis=0).astype(BF16)
-                    for part in (values, parts)
+                    jnp.concatenate([part[8 * j : 8 * j + 8] for part in parts], axis=0).astype(BF16)
+                    for parts in zip(*kept[x - 1 : x + 1])
                 ]
-                put_face(faces_y, (d, i), layer, col, hi, lo)
+                put_face(faces_y, (d, x // 2), layer, col, hi, lo)
+
+        return add
 
     def pack_block_x(c):
         for d in range(2):
@@ -314,26 +331,47 @@
     def copy_in(c, block):
         rows, y_faces = block
         for g in range(GROUPS):
-            values = [take(p0, (g, x), rows) for x in range(8)]
+            faces = put_faces_xy(g, c, y_faces)
             for x in range(8):
-                put(pc, (g, x), rows, values[x])
-            put_faces_xy(g, c, y_faces, values)
+                value = take(p0, (g, x), rows)
+                put(pc, (g, x), rows, value)
+                faces(x, value)
         pack_block_x(c)
-        for d in range(2):
-            copy_x(0, d, c).start()
 
     def copy_in_outer(k, carry):
         copy_in(k, outer_block(k))
         return carry
 
-    for copy in in_copies[3 * GROUPS :]:
+    for copy in in_copies[:GROUPS]:
         copy.wait()
     lax.fori_loop(0, 2, copy_in_outer, 0)
     copy_in(2, third_block)
     pack_y_faces()
+    copy_in(3, fourth_block)
+
+    for copy in in_copies[GROUPS:]:
+        copy.wait()
+
+    def speeds(idx, top):
+        g, x = idx // 8, lax.rem(idx, 8)
+        for y in range(8):
+            rows = slice(8 * y, 8 * y + 8)
+            total = jnp.abs(vel[0, g, x, rows, :]) + jnp.abs(vel[1, g, x, rows, :]) + jnp.abs(vel[2, g, x, rows, :])
+            top = jnp.maximum(top, total)
+        for z in range(8):
+            vz[g, x, 8 * z : 8 * z + 8, :] = vel[2, g, x, pl.ds(z, 8, stride=8), :]
+        return top
+
+    top = lax.fori_loop(0, GROUPS * 8, speeds, jnp.zeros((8, LANES), F32))
+
+    pl.semaphore_wait(barrier, len(peers))
+
+    ar_start(0, top)
     for d in range(2):
         copy_y(0, d).start()
-    copy_in(3, fourth_block)
+    for c in range(4):
+        for d in range(2):
+            copy_x(0, d, c).start()
 
     def fill(k, carry):
         for j in range(2):
@@ -434,39 +472,42 @@
                 halo[d, k, g] = halo[d, k, g] + group_of(res, g)
 
     def padded(halo, a, b, there, g, cells):
-        there_lo = pres[there, g] > 0
-        there_hi = pres[there + 1, g] > 0
-        before = [jnp.where(there_lo, halo[0, a, b, 16 * l : 16 * l + 16, :], cells[0]) for l in range(3)]
-        after = [jnp.where(there_hi, halo[1, a, b, 16 * l : 16 * l + 16, :], cells[7]) for l in range(3)]
-        return before + cells + after
+        def cell(k):
+            if 3 <= k < 11:
+                return cells(k - 3)
+            side, l, edge = (0, k, 0) if k < 3 else (1, k - 11, 7)
+            return jnp.where(pres[there + side, g] > 0, halo[side, a, b, 16 * l : 16 * l + 16, :], cells(edge))
+
+        return cell
 
     def z_lines(line, extra, half, k, halo):
         g = 2 * half + k
         for i in range(4):
-            cells = [turned_pair(pc, g, i, z) for z in range(8)]
-            values = line(padded(halo, k, i, 4, g, cells), [extra(g, i, z) for z in range(8)])
-            for z in range(8):
-                az[g, 2 * i : 2 * i + 2, 8 * z : 8 * z + 8, :] = values[z].reshape(2, 8, LANES)
+            cells = functools.partial(turned_pair, pc, g, i)
+            for z, value in enumerate(line(padded(halo, k, i, 4, g, cells), functools.partial(extra, g, i))):
+                az[g, 2 * i : 2 * i + 2, 8 * z : 8 * z + 8, :] = value.reshape(2, 8, LANES)
 
     def y_lines(line, extra, half, k, halo):
         g = 2 * half + k
         for i in range(4):
-            cells = [pair(pc, g, i, y) for y in range(8)]
-            values = line(padded(halo, k, i, 2, g, cells), [extra(g, i, y) for y in range(8)])
-            for y in range(8):
-                total = values[y] + turned_pair(az, g, i, y)
+            cells = functools.partial(pair, pc, g, i)
+            for y, value in enumerate(line(padded(halo, k, i, 2, g, cells), functools.partial(extra, g, i))):
+                total = value + turned_pair(az, g, i, y)
                 ay[g, 2 * i : 2 * i + 2, 8 * y : 8 * y + 8, :] = total.reshape(2, 8, LANES)
 
-    def x_lines(line, extra, finish, c, block, halo, k, groups=range(GROUPS)):
+    def x_lines(line, extra, finish, c, block, halo, k, groups=range(GROUPS), last=False):
         rows, y_faces = block
         ahead = [take(pc, (groups[0], x), rows) for x in range(8)]
         for g in groups:
             cells = ahead
             if g + 1 in groups:
                 ahead = [take(pc, (g + 1, x), rows) for x in range(8)]
-            values = line(padded(halo, k, g, 0, g, cells), [extra(g, x, rows) for x in range(8)])
-            fresh = [finish(g, x, rows, cells[x], values[x] + take(ay, (g, x), rows)) for x in range(8)]
-            put_faces_xy(g, c, y_faces, fresh)
+            faces = put_faces_xy(g, c, y_faces)
+            values = line(padded(halo, k, g, 0, g, cells.__getitem__), lambda x: extra(g, x, rows))
+            for x, value in enumerate(values):
+                fresh = finish(g, x, rows, cells[x], value + take(ay, (g, x), rows))
+                if not last:
+                    faces(x, fresh)
 
     def twice(body):
         def step(k, carry):
@@ -475,7 +516,14 @@
 
         lax.fori_loop(0, 2, step, 0)
 
-    def run(t, line, extra_z, extra_y, extra_x, finish, after_z=None, after_y=None):
+    def copy_out(g, start, size):
+        rows = pl.ds(start, size)
+        which = {0: 0, 48: 1, 16: 2}[start]
+        return pltpu.make_async_copy(
+            pc.at[g, :, rows], out_ref.at[:, rows, lanes(g)], out_sem.at[GROUPS * (1 + which) + g]
+        )
+
+    def run(t, line, extra_z, extra_y, extra_x, finish, after_z=None, after_y=None, last=False):
         put_faces_z()
         gather_z(0, 0, halo_za)
         gather_z(1, 0, halo_za)
@@ -522,17 +570,29 @@
         split_x(t, 1)
 
         def send_on(copies):
-            @pl.when(t + 1 < STEPS)
-            def _():
-                for copy in copies():
-                    copy.start()
+            for copy in copies():
+                copy.start()
 
         def x_outer(k):
             unpack_half_x(k, 1, halo_xb)
-            pack_block_x(lax.rem(k + 3, 4))
-            x_lines(line, extra_x, finish, k, outer_block(k), halo_xa, k)
+            if not last:
+                pack_block_x(lax.rem(k + 3, 4))
+            x_lines(line, extra_x, finish, k, outer_block(k), halo_xa, k, last=last)
 
         twice(x_outer)
+        if last:
+            out = [copy_out(g, start, 16) for start in (0, 48) for g in range(GROUPS)]
+            for copy in out:
+                copy.start()
+            x_lines(line, extra_x, finish, 2, third_block, halo_xb, 0, last=True)
+            x_lines(line, extra_x, finish, 3, fourth_block, halo_xb, 1, last=True)
+            out += [copy_out(g, 16, 32) for g in range(GROUPS)]
+            for copy in out[2 * GROUPS :]:
+                copy.start()
+            for copy in out:
+                copy.wait()
+            return
+
         send_on(lambda: [copy_x(t + 1, d, 0) for d in range(2)])
         pack_block_x(1)
         x_lines(line, extra_x, finish, 2, third_block, halo_xb, 0)
@@ -589,7 +649,7 @@
     for copy in adv_copies:
         copy.start()
 
-    def reinit_step(k, carry):
+    def reinit_step(k, last):
         def finish(g, x, rows, cell, total):
             v = take(adv, (g, x), rows)
             sign = v * lax.rsqrt(v * v + 1.0)
@@ -605,17 +665,12 @@
             lambda g, i, y: pair(sgn, g, i, y),
             lambda g, x, rows: take(sgn, (g, x), rows),
             finish,
+            last=last,
         )
-        return carry
-
-    lax.fori_loop(0, REINIT, reinit_step, 0)
-
-    out_copies = [
-        pltpu.make_async_copy(pc.at[g], out_ref.at[:, :, lanes(g)], out_sem.at[GROUPS + g]) for g in range(GROUPS)
-    ]
-    for copy in out_copies:
-        copy.start()
-    for copy in adv_copies + out_copies:
+
+    for k in range(REINIT):
+        reinit_step(k, k == REINIT - 1)
+    for copy in adv_copies:
         copy.wait()
 
 
@@ -684,7 +739,7 @@
                 pltpu.VMEM((max(1, n_band // low - 1), 8, LANES), F32),
                 pltpu.VMEM((16, LANES), F32),
                 pltpu.SemaphoreType.DMA((16,)),
-                pltpu.SemaphoreType.DMA((2 * GROUPS,)),
+                pltpu.SemaphoreType.DMA((5 * GROUPS,)),
                 pltpu.SemaphoreType.DMA((2, 4)),
                 pltpu.SemaphoreType.DMA((STEPS, 2, 4)),
                 pltpu.SemaphoreType.DMA((2,)),

time: 65.3 us -> 61.5 us (0.942)
  Pallas kernels: 64.4 us -> 60.5 us
    pallas_call x1, Pallas kernels: 62 us -> 58.1 us  [local(): pl.pallas_call(functools.partial(kernel, n_band, n_sub, low), out_shape=(...]
where the time goes in v4:
time: 61.5 us; the launch traced here: 61.3 us
  Pallas kernels  60.5 us (98%)
  between operations  0.8 us (1%)
    pallas_call x1, Pallas kernels, local(): pl.pallas_call(functools.partial(kernel, n_band, n_sub, low), out_shape=(...  58.1 us
    pallas_call x1, Pallas kernels, local(): pl.pallas_call(hand_over, out_shape=(whole, whole), in_specs=[anywhere, a...  2.4 us

profile of v4, /device:TPU:0, one launch (start us, length us, event | category | flops | bytes accessed | tf_op | source)
XLA Modules:
  0.0 61.3 jit_solution(6342048784072458109)
XLA Ops:
  0.6 58.1 %shard_map.50 = (f32[8,64,512]{2,1,0:T(8,128)}, f32[8,64,512]{2,1,0:T(8,128)}) custom-call(f32[8,64,512]{2,1,0:T(8,128)} %bitcast.5, f32[3,8,64,512]{3,2,1,0:T(8,128)} %bitcast.4, s32[6,512]{1,0:T(8,128)} %nb_ref.1), custom_call_target="tpu_custom_call" | custom-call | tf_op jit(solution)/shard_map/pallas_call | solution.py:701
  58.7 2.4 %shard_map.51 = (f32[8,64,512]{2,1,0:T(8,128)}, f32[8,64,512]{2,1,0:T(8,128)}) custom-call(f32[8,64,512]{2,1,0:T(8,128)} %get-tuple-element.6.a_ref, f32[8,64,512]{2,1,0:T(8,128)} %get-tuple-element.7.b_ref), custom_call_target="tpu_custom_call" | custom-call | tf_op jit(solution)/shard_map/pallas_call | solution.py:754

commit v5 on v4

--- a/solution.py
+++ b/solution.py
@@ -97,7 +97,7 @@
 def advect_line(cell, flow_of):
     get = Line(cell).get
     for c in range(8):
-        flow = flow_of(c)
+        flow, size = flow_of(c)
         up = flow > 0
         ra = recip(jnp.where(up, get("ind_a", c), get("ind_c", c + 3)))
         rb = recip(jnp.where(up, get("ind_b", c + 1), get("ind_b", c + 2)))
@@ -109,7 +109,7 @@
         num = wa * (far + far) + wc * get("fourth", c + 2)
         corr = num * recip(wa + wb + wc)
         linear = 3.0 * (get("cell", c + 4) - get("cell", c + 2)) - jnp.where(up, get("third", c + 1), get("third", c + 2))
-        yield flow * linear - jnp.abs(flow) * corr
+        yield flow * linear - size * corr
 
 
 def reinit_line(cell, sign_of):
@@ -146,7 +146,7 @@
 def kernel(
     n_band, n_sub, low,
     ls_ref, vel_ref, nb_ref, adv_out, out_ref,
-    p0, pc, adv, sgn, vel, vz, az, ay,
+    p0, pc, adv, sgn, vel, vz, size, az, ay,
     halo_xa, halo_xb, halo_ya, halo_yb, halo_za, halo_zb, faces_x, faces_y, faces_z, came_x, came_y,
     local_m, pack_x, pack_y, unpack_x, unpack_y, tri, pres,
     nb_s, ids_s, krow, kcol, send_x, send_y, recv_x, recv_y, ar_send, ar_near, ar_far, step_s,
@@ -356,10 +356,14 @@
         g, x = idx // 8, lax.rem(idx, 8)
         for y in range(8):
             rows = slice(8 * y, 8 * y + 8)
-            total = jnp.abs(vel[0, g, x, rows, :]) + jnp.abs(vel[1, g, x, rows, :]) + jnp.abs(vel[2, g, x, rows, :])
-            top = jnp.maximum(top, total)
+            sizes = [jnp.abs(vel[k, g, x, rows, :]) for k in range(3)]
+            top = jnp.maximum(top, sizes[0] + sizes[1] + sizes[2])
+            size[0, g, x, rows, :] = sizes[0]
+            size[1, g, x, rows, :] = sizes[1]
         for z in range(8):
-            vz[g, x, 8 * z : 8 * z + 8, :] = vel[2, g, x, pl.ds(z, 8, stride=8), :]
+            turned = vel[2, g, x, pl.ds(z, 8, stride=8), :]
+            vz[g, x, 8 * z : 8 * z + 8, :] = turned
+            size[2, g, x, 8 * z : 8 * z + 8, :] = jnp.abs(turned)
         return top
 
     top = lax.fori_loop(0, GROUPS * 8, speeds, jnp.zeros((8, LANES), F32))
@@ -418,8 +422,8 @@
     def pair(ref, g, i, k):
         return ref[g, 2 * i : 2 * i + 2, 8 * k : 8 * k + 8, :].reshape(16, LANES)
 
-    def put_faces_z():
-        for g in range(GROUPS):
+    def put_faces_z(groups):
+        for g in groups:
             col = pl.ds(g * LANES, LANES)
             for i in range(4):
                 for d, start in ((0, 5), (1, 0)):
@@ -472,11 +476,15 @@
                 halo[d, k, g] = halo[d, k, g] + group_of(res, g)
 
     def padded(halo, a, b, there, g, cells):
+        masks = {}
+
         def cell(k):
             if 3 <= k < 11:
                 return cells(k - 3)
             side, l, edge = (0, k, 0) if k < 3 else (1, k - 11, 7)
-            return jnp.where(pres[there + side, g] > 0, halo[side, a, b, 16 * l : 16 * l + 16, :], cells(edge))
+            if side not in masks:
+                masks[side] = pres[there + side, g] > 0, cells(edge)
+            return jnp.where(masks[side][0], halo[side, a, b, 16 * l : 16 * l + 16, :], masks[side][1])
 
         return cell
 
@@ -524,7 +532,6 @@
         )
 
     def run(t, line, extra_z, extra_y, extra_x, finish, after_z=None, after_y=None, last=False):
-        put_faces_z()
         gather_z(0, 0, halo_za)
         gather_z(1, 0, halo_za)
 
@@ -537,9 +544,9 @@
             z_lines(line, extra_z, 1, k, halo_zb)
 
         twice(z_first)
-        twice(z_second)
         if after_z is not None:
             after_z()
+        twice(z_second)
         for d in range(2):
             copy_y(t, d).wait()
         split_y(t)
@@ -602,9 +609,13 @@
         send_on(lambda: [copy_y(t + 1, d) for d in range(2)])
         pack_block_x(2)
         x_lines(line, extra_x, finish, 3, fourth_block, halo_xb, 1, range(2, 4))
+        put_faces_z(range(2))
         send_on(lambda: [copy_x(t + 1, d, 2) for d in range(2)])
         pack_block_x(3)
+        put_faces_z(range(2, 4))
         send_on(lambda: [copy_x(t + 1, d, 3) for d in range(2)])
+
+    put_faces_z(range(GROUPS))
 
     def advect_step(t, carry):
         def after_z():
@@ -632,9 +643,9 @@
         run(
             t,
             advect_line,
-            lambda g, i, z: pair(vz, g, i, z),
-            lambda g, i, y: pair(vel.at[1], g, i, y),
-            lambda g, x, rows: take(vel, (0, g, x), rows),
+            lambda g, i, z: (pair(vz, g, i, z), pair(size.at[2], g, i, z)),
+            lambda g, i, y: (pair(vel.at[1], g, i, y), pair(size.at[1], g, i, y)),
+            lambda g, x, rows: (take(vel, (0, g, x), rows), take(size, (0, g, x), rows)),
             finish,
             after_z,
             after_y,
@@ -692,7 +703,7 @@
 
 def solution(mesh):
     n_band, n_sub = mesh.shape["band"], mesh.shape["sub"]
-    low = min(4, n_band)
+    low = min(2, n_band)
     cells = (GROUPS, 8, 64, LANES)
 
     def local(level_set, velocity, neighbours):
@@ -710,6 +721,7 @@
                 pltpu.VMEM(cells, F32),
                 pltpu.VMEM((3,) + cells, F32),
                 pltpu.VMEM(cells, F32),
+                pltpu.VMEM((3,) + cells, F32),
                 pltpu.VMEM(cells, F32),
                 pltpu.VMEM(cells, F32),
                 *[pltpu.VMEM((2, 2, GROUPS, BLOCK, LANES), F32)] * 2,

time: 61.5 us -> 60.6 us (0.985)
  Pallas kernels: 60.5 us -> 59.6 us
    pallas_call x1, Pallas kernels: 58.1 us -> 57.2 us  [local(): pl.pallas_call(functools.partial(kernel, n_band, n_sub, low), out_shape=(...]
where the time goes in v5:
time: 60.6 us; the launch traced here: 60.4 us
  Pallas kernels  59.6 us (98%)
  between operations  0.8 us (1%)
    pallas_call x1, Pallas kernels, local(): pl.pallas_call(functools.partial(kernel, n_band, n_sub, low), out_shape=(...  57.2 us
    pallas_call x1, Pallas kernels, local(): pl.pallas_call(hand_over, out_shape=(whole, whole), in_specs=[anywhere, a...  2.4 us

profile of v5, /device:TPU:0, one launch (start us, length us, event | category | flops | bytes accessed | tf_op | source)
XLA Modules:
  0.0 60.4 jit_solution(1488942856480006421)
XLA Ops:
  0.6 57.2 %shard_map.50 = (f32[8,64,512]{2,1,0:T(8,128)}, f32[8,64,512]{2,1,0:T(8,128)}) custom-call(f32[8,64,512]{2,1,0:T(8,128)} %bitcast.5, f32[3,8,64,512]{3,2,1,0:T(8,128)} %bitcast.4, s32[6,512]{1,0:T(8,128)} %nb_ref.1), custom_call_target="tpu_custom_call" | custom-call | tf_op jit(solution)/shard_map/pallas_call | solution.py:712
  57.9 2.4 %shard_map.51 = (f32[8,64,512]{2,1,0:T(8,128)}, f32[8,64,512]{2,1,0:T(8,128)}) custom-call(f32[8,64,512]{2,1,0:T(8,128)} %get-tuple-element.6.a_ref, f32[8,64,512]{2,1,0:T(8,128)} %get-tuple-element.7.b_ref), custom_call_target="tpu_custom_call" | custom-call | tf_op jit(solution)/shard_map/pallas_call | solution.py:766

commit v6 on v5

--- a/solution.py
+++ b/solution.py
@@ -441,6 +441,15 @@
             for g in range(2):
                 halo[d, g, i] = group_of(res, g)
 
+    def gather_z_from(source):
+        columns = slice(2 * source * LANES, 2 * (source + 1) * LANES)
+        for d in range(2):
+            faces = faces_z[d].reshape(8 * BLOCK, TILES_DEV)[:, columns]
+            for i, res in enumerate(two_part_dot(faces, local_m[4 + d, columns, : 2 * LANES])):
+                for g in range(2):
+                    part = group_of(res, g)
+                    halo_za[d, g, i] = halo_za[d, g, i] + part if source else part
+
     def gather_y(d):
         for i, res in enumerate(two_part_dot(faces_y[d].reshape(8 * BLOCK, TILES_DEV), local_m[2 + d])):
             for g in range(GROUPS):
@@ -532,8 +541,7 @@
         )
 
     def run(t, line, extra_z, extra_y, extra_x, finish, after_z=None, after_y=None, last=False):
-        gather_z(0, 0, halo_za)
-        gather_z(1, 0, halo_za)
+        gather_z_from(1)
 
         def z_first(k):
             gather_z(k, 1, halo_zb)
@@ -608,14 +616,16 @@
         x_lines(line, extra_x, finish, 3, fourth_block, halo_xb, 1, range(2))
         send_on(lambda: [copy_y(t + 1, d) for d in range(2)])
         pack_block_x(2)
+        put_faces_z(range(2))
+        gather_z_from(0)
         x_lines(line, extra_x, finish, 3, fourth_block, halo_xb, 1, range(2, 4))
-        put_faces_z(range(2))
         send_on(lambda: [copy_x(t + 1, d, 2) for d in range(2)])
         pack_block_x(3)
         put_faces_z(range(2, 4))
         send_on(lambda: [copy_x(t + 1, d, 3) for d in range(2)])
 
     put_faces_z(range(GROUPS))
+    gather_z_from(0)
 
     def advect_step(t, carry):
         def after_z():

time: 60.6 us -> 60.6 us (level)
  no operation moved by 1% of the time
where the time goes in v6:
time: 60.6 us; the launch traced here: 60.5 us
  Pallas kernels  59.7 us (99%)
  between operations  0.8 us (1%)
    pallas_call x1, Pallas kernels, local(): pl.pallas_call(functools.partial(kernel, n_band, n_sub, low), out_shape=(...  57.3 us
    pallas_call x1, Pallas kernels, local(): pl.pallas_call(hand_over, out_shape=(whole, whole), in_specs=[anywhere, a...  2.4 us

profile of v6, /device:TPU:0, one launch (start us, length us, event | category | flops | bytes accessed | tf_op | source)
XLA Modules:
  0.0 60.5 jit_solution(16921997068537995383)
XLA Ops:
  0.6 57.3 %shard_map.50 = (f32[8,64,512]{2,1,0:T(8,128)}, f32[8,64,512]{2,1,0:T(8,128)}) custom-call(f32[8,64,512]{2,1,0:T(8,128)} %bitcast.5, f32[3,8,64,512]{3,2,1,0:T(8,128)} %bitcast.4, s32[6,512]{1,0:T(8,128)} %nb_ref.1), custom_call_target="tpu_custom_call" | custom-call | tf_op jit(solution)/shard_map/pallas_call | solution.py:722
  57.9 2.4 %shard_map.51 = (f32[8,64,512]{2,1,0:T(8,128)}, f32[8,64,512]{2,1,0:T(8,128)}) custom-call(f32[8,64,512]{2,1,0:T(8,128)} %get-tuple-element.6.a_ref, f32[8,64,512]{2,1,0:T(8,128)} %get-tuple-element.7.b_ref), custom_call_target="tpu_custom_call" | custom-call | tf_op jit(solution)/shard_map/pallas_call | solution.py:776
